TPU v7x, 32 devices: a whole 2x2x4 slice. The times are simulated.
32 devices in a mesh: seq: 8 (over z, y), head: 4 (over x, core).
Axes of the slice: x: 2, y: 2, z: 4, core: 2. Of those that a mesh axis runs over, the one named last changes fastest.
Arguments:
- query_in: bfloat16 [2048, 4096], P('seq', 'head'), may hold values from -6 to 6
- key_in: bfloat16 [2048, 4096], P('seq', 'head'), may hold values from -6 to 6
- value_in: bfloat16 [2048, 4096], P('seq', 'head')
- out_grad: bfloat16 [2048, 4096], P('seq', 'head'), may hold values from -6 to 6
- norm_gain: float32 [4096], P('head'), may hold values from 0.5 to 1.5
- doc_ids: int32 [2048], P('seq'), may hold values from 0 to 7, as said below
- start_group: int32 [8], replicated, may hold values from 0 to 6, as said below
Outputs:
- normed: bfloat16 [2048, 4096], P('seq', 'head')
- grad_query: bfloat16 [2048, 4096], P('seq', 'head')
- grad_key: bfloat16 [2048, 4096], P('seq', 'head')
- grad_value: bfloat16 [2048, 4096], P('seq', 'head')
Inputs may be any that keep to these rules, and one draw needn't show every extreme that they name: `doc_ids`: 0 at the first token, never falling, one more at each document start. `start_group`: entry c is the block in which the document holding block c's first token begins; it agrees with doc_ids.
All inputs are finite; a program needn't handle non-finite values.
Results may differ from a plain program's by a relative error of at most 0.0058.
Values may be sent and summed in bfloat16 or wider, within the bound.
No kernel may reach another device: no remote copies, remote signals or barrier semaphores. Data moves between devices by JAX's collectives and lax.ppermute only.
A program may use at most 128 MiB of HBM per device.

v0:
```python
import jax
import jax.numpy as jnp
from jax import lax
from jax.sharding import PartitionSpec as P

H = 32
HD = 128


epsilon = 1e-06


def prefix(x, axis, combine, identity, reverse):
    length, mine = (lax.axis_size(axis), lax.axis_index(axis))
    everything = jax.tree.map(lambda part: lax.all_gather(part, axis), x)
    start = jax.tree.map(
        lambda part, zero: jnp.broadcast_to(jnp.asarray(zero, part.dtype), part.shape), x, identity
    )

    def lap(k, before):
        at = length - 1 - k if reverse else k
        reached = at > mine if reverse else at < mine
        new = combine(before, jax.tree.map(lambda part: part[at], everything))
        return jax.tree.map(lambda a, b: jnp.where(reached, a, b), new, before)

    return lax.fori_loop(0, length, lap, start)


def segment_join(earlier, later):
    return (
        jnp.maximum(earlier[0], later[0]),
        jnp.where(later[0] > 0.5, later[1], earlier[1] + later[1]),
    )


def local(query_in, key_in, value_in, out_grad, norm_gain, doc_ids, start_group):
    length = query_in.shape[0]
    heads_here = query_in.shape[1] // HD
    width = H * HD
    groups = lax.axis_size("seq")
    group_index = lax.axis_index("seq")
    query_h = query_in.reshape(length, heads_here, HD)
    key_h = key_in.reshape(length, heads_here, HD)
    value_h = value_in.reshape(length, heads_here, HD)
    grad_h = out_grad.reshape(length, heads_here, HD)
    gain_heads = norm_gain.reshape(heads_here, HD)
    first_doc = doc_ids == doc_ids[0]
    last_doc = doc_ids == doc_ids[length - 1]
    first_f = first_doc.astype(jnp.float32)[:, None, None]
    last_f = last_doc.astype(jnp.float32)[:, None, None]
    causal = jnp.arange(length)[:, None] >= jnp.arange(length)[None, :]
    same_doc = causal & (doc_ids[:, None] == doc_ids[None, :])
    local_change = jnp.any(doc_ids[1:] != doc_ids[:-1])
    own_start = start_group[group_index]
    next_start = start_group[jnp.minimum(group_index + 1, groups - 1)]
    tail_state = jnp.einsum(
        "tha,thb->hab",
        key_h * last_doc.astype(jnp.bfloat16)[:, None, None],
        value_h,
        preferred_element_type=jnp.float32,
    )
    restart = jnp.where(local_change | (own_start == group_index), 1.0, 0.0).astype(jnp.float32)
    scanned = prefix(
        (restart, tail_state),
        "seq",
        segment_join,
        (jnp.zeros((), jnp.float32), jnp.zeros_like(tail_state)),
        False,
    )
    carry_b = jnp.where(own_start == group_index, 0.0, scanned[1]).astype(jnp.bfloat16)
    scores = jnp.einsum("tha,uha->htu", query_h, key_h, preferred_element_type=jnp.float32)
    weights = jnp.where(same_doc[None], scores, 0.0).astype(jnp.bfloat16)
    attended = jnp.einsum("htu,uhb->thb", weights, value_h, preferred_element_type=jnp.float32)
    attended = attended + first_f * jnp.einsum(
        "tha,hab->thb", query_h, carry_b, preferred_element_type=jnp.float32
    )
    square_part = jnp.sum(attended * attended, axis=(1, 2))
    cross_part = jnp.sum(gain_heads * grad_h * attended, axis=(1, 2))
    square_total = lax.psum(square_part, "head")
    inverse_rms = lax.rsqrt(square_total / width + epsilon)
    normed = (attended * inverse_rms[:, None, None] * gain_heads).astype(jnp.bfloat16)
    cross_total = lax.psum(cross_part, "head")
    grad_attended = (
        inverse_rms[:, None, None] * gain_heads * grad_h
        - (inverse_rms**3 * cross_total / width)[:, None, None] * attended
    ).astype(jnp.bfloat16)
    head_state = jnp.einsum(
        "tha,thb->hab",
        query_h * first_doc.astype(jnp.bfloat16)[:, None, None],
        grad_attended,
        preferred_element_type=jnp.float32,
    )
    closing = jnp.where(local_change | (next_start == group_index + 1), 1.0, 0.0).astype(
        jnp.float32
    )
    scanned_back = prefix(
        (closing, head_state),
        "seq",
        segment_join,
        (jnp.zeros((), jnp.float32), jnp.zeros_like(head_state)),
        True,
    )
    back_b = jnp.where(next_start == group_index + 1, 0.0, scanned_back[1]).astype(jnp.bfloat16)
    grad_scores = jnp.where(
        same_doc[None],
        jnp.einsum("tha,uha->htu", grad_attended, value_h, preferred_element_type=jnp.float32),
        0.0,
    ).astype(jnp.bfloat16)
    grad_query = jnp.einsum("htu,uha->tha", grad_scores, key_h, preferred_element_type=jnp.float32)
    grad_query = grad_query + first_f * jnp.einsum(
        "thb,hab->tha", grad_attended, carry_b, preferred_element_type=jnp.float32
    )
    grad_key = jnp.einsum("htu,tha->uha", grad_scores, query_h, preferred_element_type=jnp.float32)
    grad_key = grad_key + last_f * jnp.einsum(
        "uhb,hab->uha", value_h, back_b, preferred_element_type=jnp.float32
    )
    grad_value = jnp.einsum(
        "htu,thb->uhb", weights, grad_attended, preferred_element_type=jnp.float32
    )
    grad_value = grad_value + last_f * jnp.einsum(
        "uha,hab->uhb", key_h, back_b, preferred_element_type=jnp.float32
    )
    shape = (length, heads_here * HD)
    return (
        normed.reshape(shape),
        grad_query.astype(jnp.bfloat16).reshape(shape),
        grad_key.astype(jnp.bfloat16).reshape(shape),
        grad_value.astype(jnp.bfloat16).reshape(shape),
    )


def solution(mesh):
    placed = (
        P("seq", "head"),
        P("seq", "head"),
        P("seq", "head"),
        P("seq", "head"),
        P("head"),
        P("seq"),
        P(),
    )
    return jax.shard_map(
        local,
        mesh=mesh,
        in_specs=placed,
        out_specs=(P("seq", "head"), P("seq", "head"), P("seq", "head"), P("seq", "head")),
        check_vma=False,
    )
```

profile of v0, /device:TPU:0, one launch (start us, length us, event | category | flops | bytes accessed | tf_op | source)
XLA Modules:
  0.0 224.9 jit_solution(15133744079087134640)
XLA Ops:
  7.2 1.3 fusion.41
  10.1 1.3 fusion.37
  18.7 23.6 %all-reduce.2 = (f32[8]{0:T(128)S(1)}, f32[8]{0:T(128)S(1)}) all-reduce(f32[8]{0:T(128)S(1)} %dynamic-update-slice, f32[8]{0:T(128)S(1)} %dynamic-update-slice.1), channel_id=1, replica_groups=mesh['seq'=8,'head'=4] {'seq'}, use_global_device_ids=true, to_apply=%add | all-reduce | flops 16 | bytes 128
  42.5 1.4 copy.40
  45.5 1.5 convolution_bitcast_fusion.2
  47.0 42.1 %all-gather.5.cloned.1.call-done = f32[64,128,128]{2,1,0:T(8,128)} async-done(((f32[8,128,128]{2,1,0:T(8,128)}), f32[64,128,128]{2,1,0:T(8,128)}) %all-gather.5.cloned.1.call-update) | async-done | bytes 4194320 | tf_op jit(solution)/shard_map/all_gather | solution.py:15
  89.2 20.5 %while.30 = (s32[]{:T(128)}, f32[8,128,128]{2,1,0:T(8,128)S(1)}, s32[]{:T(128)}, f32[8]{0:T(128)S(1)}, f32[8,8,128,128]{3,2,1,0:T(8,128)}, /*index=5*/s32[]{:T(128)}, s32[]{:T(128)}, f32[1]{0:T(128)}) while((s32[]{:T(128)}, f32[8,128,128]{2,1,0:T(8,128)S(1)}, s32[]{:T(128)}, f32[8]{0:T(128)S(1)}, f32[8,8,128,128]{3,2,1,0:T(8,128)}, ...), condition=%wide.region_2.3_spmd.clone, body=%wide.region_1.2_spmd.clone.sunk | while | flops 524293 | bytes 1573003 | solution.py:26
  90.4 1.3 fusion.64
  93.0 1.3 fusion.64
  95.5 1.3 fusion.64
  98.1 1.3 fusion.64
  100.7 1.3 fusion.64
  103.2 1.3 fusion.64
  105.8 1.3 fusion.64
  108.4 1.3 fusion.64
  109.7 2.7 %multiply_reduce_fusion = (f32[256]{0:T(256)S(1)}, f32[256]{0:T(256)S(1)}, f32[256,8,128]{0,2,1:T(8,128)}) fusion(f32[8,128]{1,0:T(8,128)S(1)} %bitcast.116, f32[256,1024]{0,1:T(8,128)S(1)} %copy.40, f32[256,8,128]{0,2,1:T(8,128)} %convolution_bitcast_fusion.2, bf16[256,8,128]{0,2,1:T(8,128)(2,1)S(1)} %bitcast.105, ...), kind=kOutput, calls=%fused_computation.24 | convolution fusion | flops 69074432 | bytes 4201473 | tf_op jit(solution)/shard_map/tha,hab->thb/dot_general | solution.py:74
  112.4 5.6 %all-reduce.3 = (f32[256]{0:T(256)S(1)}, f32[256]{0:T(256)S(1)}) all-reduce(f32[256]{0:T(256)S(1)} %get-tuple-element.277, f32[256]{0:T(256)S(1)} %get-tuple-element.276), channel_id=1, replica_groups=mesh['seq'=8,'head'=4] {'head'}, use_global_device_ids=true, to_apply=%region_4.5 | all-reduce | flops 512 | bytes 4096 | tf_op jit(solution)/shard_map/psum | solution.py:79
  118.1 2.3 %subtract_convert_fusion = (bf16[256,8,128]{0,2,1:T(8,128)(2,1)S(1)}, bf16[256,8,128]{0,2,1:T(8,128)(2,1)}) fusion(f32[256,8,128]{0,2,1:T(8,128)} %get-tuple-element.314, f32[256,8,128]{0,2,1:T(8,128)S(1)} %bitcast.103, f32[256]{0:T(256)S(1)} %get-tuple-element.308, f32[8,128]{1,0:T(8,128)S(1)} %bitcast.117, f32[256]{0:T(256)S(1)} %get-tuple-element.309), kind=kLoop, calls=%fused_computation.23 | loop fusion | flops 2097152 | bytes 3151872 | tf_op jit(solution)/shard_map/convert_element_type | solution.py:86
  124.6 2.1 copy.52
  128.4 65.2 %all-gather.7.cloned.1.call-done = f32[64,128,128]{2,1,0:T(8,128)} async-done(((f32[8,128,128]{2,1,0:T(8,128)}), f32[64,128,128]{2,1,0:T(8,128)}) %all-gather.7.cloned.1.call-update) | async-done | bytes 4194320 | tf_op jit(solution)/shard_map/all_gather | solution.py:15
  193.6 20.5 %while.31 = (s32[]{:T(128)}, f32[8,128,128]{2,1,0:T(8,128)S(1)}, s32[]{:T(128)}, f32[8]{0:T(128)S(1)}, f32[8,8,128,128]{3,2,1,0:T(8,128)}, /*index=5*/s32[]{:T(128)}, s32[]{:T(128)}, s32[]{:T(128)}, s32[]{:T(128)}, f32[1]{0:T(128)}) while((s32[]{:T(128)}, f32[8,128,128]{2,1,0:T(8,128)S(1)}, s32[]{:T(128)}, f32[8]{0:T(128)S(1)}, ...), condition=%wide.region_8.9_spmd.clone, body=%wide.region_7.8_spmd.clone.sunk | while | flops 524297 | bytes 1573065 | solution.py:26
  194.8 1.3 fusion.65
  197.4 1.3 fusion.65
  214.1 1.6 fusion.11
  (86 shorter events, 33.3 us)
Async XLA Ops:
  7.2 4.3 %copy-start = (bf16[256,1024]{1,0:T(8,128)(2,1)S(1)}, bf16[256,1024]{1,0:T(8,128)(2,1)}, u32[]{:S(2)}) copy-start(bf16[256,1024]{1,0:T(8,128)(2,1)} %param.13) | copy-start | bytes 1572868
  7.2 2.9 %copy-start.13 = (s32[256]{0:T(256)S(1)}, s32[256]{0:T(256)}, u32[]{:S(2)}) copy-start(s32[256]{0:T(256)} %param.16) | copy-start | bytes 3076
  7.2 82.0 %all-gather.5.cloned.1.call-start = ((), (), s32[]{:S(2)}) async-start(), calls=%async_computation | async-start | bytes 4718592 | tf_op jit(solution)/shard_map/all_gather | solution.py:15
  8.6 4.1 %copy-start.15 = (s32[8]{0:T(128)S(1)}, s32[8]{0:T(128)}, u32[]{:S(2)}) copy-start(s32[8]{0:T(128)} %param.17) | copy-start | bytes 100
  8.6 8.0 %copy-start.16 = (u32[32]{0:T(128)S(1)}, u32[32]{0:T(128)}, u32[]{:S(2)}) copy-start(u32[32]{0:T(128)} %constant.110) | copy-start | bytes 388
  8.6 33.7 %copy-start.12 = (bf16[256,1024]{1,0:T(8,128)(2,1)S(1)}, bf16[256,1024]{1,0:T(8,128)(2,1)}, u32[]{:S(2)}) copy-start(bf16[256,1024]{1,0:T(8,128)(2,1)} %param.11) | copy-start | bytes 1572868
  10.1 32.2 %copy-start.3 = (bf16[256,8,128]{0,2,1:T(8,128)(2,1)}, bf16[256,8,128]{0,2,1:T(8,128)(2,1)S(1)}, u32[]{:S(2)}) copy-start(bf16[256,8,128]{0,2,1:T(8,128)(2,1)S(1)} %copy.36) | copy-start | bytes 1572868
  11.5 32.6 %copy-start.9 = (bf16[256,1024]{1,0:T(8,128)(2,1)S(1)}, bf16[256,1024]{1,0:T(8,128)(2,1)}, u32[]{:S(2)}) copy-start(bf16[256,1024]{1,0:T(8,128)(2,1)} %param.12) | copy-start | bytes 1572868
  12.6 181.0 %all-gather.7.cloned.1.call-start = ((), (), s32[]{:S(2)}) async-start(), calls=%async_computation.1 | async-start | bytes 4718592 | tf_op jit(solution)/shard_map/all_gather | solution.py:15
  42.5 77.9 %copy-start.1 = (bf16[256,1024]{0,1:T(8,128)(2,1)}, bf16[256,1024]{0,1:T(8,128)(2,1)S(1)}, u32[]{:S(2)}) copy-start(bf16[256,1024]{0,1:T(8,128)(2,1)S(1)} %copy.60) | copy-start | bytes 1572868
  44.6 1.0 copy-start.5
  89.2 20.5 %copy-start.14 = (f32[1024]{0:T(1024)S(1)}, f32[1024]{0:T(1024)}, u32[]{:S(2)}) copy-start(f32[1024]{0:T(1024)} %param.15) | copy-start | bytes 12292
  120.4 1.1 copy-start.11
  121.5 1.5 copy-start.4
  123.0 1.6 copy-start.7
  123.5 3.2 %copy-start.6 = (bf16[8,256,256]{2,1,0:T(8,128)(2,1)S(1)}, bf16[8,256,256]{2,1,0:T(8,128)(2,1)}, u32[]{:S(2)}) copy-start(bf16[8,256,256]{2,1,0:T(8,128)(2,1)} %copy-done.5) | copy-start | bytes 3145732
  124.6 3.4 %copy-start.2 = (bf16[256,1024]{0,1:T(8,128)(2,1)S(1)}, bf16[256,1024]{0,1:T(8,128)(2,1)}, u32[]{:S(2)}) copy-start(bf16[256,1024]{0,1:T(8,128)(2,1)} %copy-done.1) | copy-start | bytes 1572868
  126.7 1.4 copy-start.8
  193.6 20.6 %copy-start.10 = (bf16[256,1024]{1,0:T(8,128)(2,1)S(1)}, bf16[256,1024]{1,0:T(8,128)(2,1)}, u32[]{:S(2)}) copy-start(bf16[256,1024]{1,0:T(8,128)(2,1)} %param.12) | copy-start | bytes 1572868
Sparse Core Ops, SparseCore 0:
  12.7 76.4 all-gather.4
  121.6 71.9 all-gather.6
where the time goes:
time: 226 us; the launch traced here: 225 us
  waiting for transfers between devices  107 us (47%)
  blocking collectives  29.2 us (13%)
  other arithmetic  25.3 us (11%)
  local copies, waits for them, and re-layouts  22.8 us (10%)
  between operations  16.9 us (7%)
  matrix products  12.4 us (5%)
  loops' own time  10.8 us (5%)
    all_gather x2, waiting for transfers between devices, prefix(): everything = jax.tree.map(lambda part: lax.all_gather(part, axis), x)  107 us
    unnamed x1, blocking collectives  23.6 us
    select_n x16, other arithmetic, lap(): return jax.tree.map(lambda a, b: jnp.where(reached, a, b), new, before)  20.8 us
    another operation x2, loops' own time, prefix(): return lax.fori_loop(0, length, lap, start)  10.8 us
    unnamed x44, local copies, waits for them, and re-layouts  9.52 us
    dynamic_slice x16, local copies, waits for them, and re-layouts, lap(): new = combine(before, jax.tree.map(lambda part: part[at], everything))  9.37 us
    psum x1, blocking collectives, local(): square_total = lax.psum(square_part, 'head')  5.63 us
  transfers between devices with their start and end apart: 2, of which 2 were waited for; matrix products, arithmetic and copies ran while one was open for 6% of the time, Pallas kernels for 0%

commit v1 on v0

v1 whole, which is shorter than its diff:
```python
import functools

import jax
import jax.numpy as jnp
from jax import lax
from jax.experimental import pallas as pl
from jax.experimental.pallas import tpu as pltpu
from jax.sharding import PartitionSpec as P

H = 32
HD = 128
WIDTH = H * HD

epsilon = 1e-06

f32 = jnp.float32
bf16 = jnp.bfloat16


def dot(a, b, da, db):
    return lax.dot_general(a, b, (((da,), (db,)), ((), ())), preferred_element_type=f32)


def head_cols(h):
    return slice(h * HD, (h + 1) * HD)


def column(row):
    n = row.shape[1]
    at = lax.broadcasted_iota(jnp.int32, (n, n), 0) == lax.broadcasted_iota(jnp.int32, (n, n), 1)
    return jnp.sum(jnp.where(at, row, 0.0), axis=1, keepdims=True)


def as_row(col):
    n = col.shape[0]
    at = lax.broadcasted_iota(jnp.int32, (n, n), 0) == lax.broadcasted_iota(jnp.int32, (n, n), 1)
    return jnp.sum(jnp.where(at, col, 0.0), axis=0, keepdims=True)


def ids_of(ids_ref):
    row = ids_ref[...].astype(f32)
    return row, column(row)


def first_of(row, col):
    return (col == row[:, :1]).astype(f32)


def last_of(row, col):
    return (col == row[:, -1:]).astype(f32)


def wide(col, dtype=bf16):
    return jnp.broadcast_to(col, (col.shape[0], HD)).astype(dtype)


def tail_kernel(ids_ref, k_ref, v_ref, tail_ref):
    row, col = ids_of(ids_ref)
    last = wide(last_of(row, col))
    for h in range(tail_ref.shape[0]):
        tail_ref[h] = dot(k_ref[:, head_cols(h)] * last, v_ref[:, head_cols(h)], 0, 0).astype(bf16)


def local_kernel(ids_ref, q_ref, k_ref, v_ref, att_ref):
    row, col = ids_of(ids_ref)
    n = row.shape[1]
    t = lax.broadcasted_iota(jnp.int32, (n, n), 0)
    u = lax.broadcasted_iota(jnp.int32, (n, n), 1)
    same = (u <= t) & (col == row)
    for h in range(q_ref.shape[1] // HD):
        c = head_cols(h)
        w = jnp.where(same, dot(q_ref[:, c], k_ref[:, c], 1, 1), 0.0).astype(bf16)
        att_ref[:, c] = dot(w, v_ref[:, c], 1, 0)


def attend_kernel(ids_ref, att_ref, q_ref, g_ref, gain_ref, carry_ref, out_ref, sums_ref):
    row, col = ids_of(ids_ref)
    first = wide(first_of(row, col))
    square = jnp.zeros((row.shape[1], HD), f32)
    cross = jnp.zeros((row.shape[1], HD), f32)
    for h in range(q_ref.shape[1] // HD):
        c = head_cols(h)
        att = att_ref[:, c] + dot(q_ref[:, c] * first, carry_ref[h], 1, 0)
        out_ref[:, c] = att
        square = square + att * att
        cross = cross + gain_ref[:, c] * g_ref[:, c].astype(f32) * att
    sums_ref[0:1, :] = as_row(jnp.sum(square, axis=1, keepdims=True))
    sums_ref[1:2, :] = as_row(jnp.sum(cross, axis=1, keepdims=True))


def scales(sum_refs):
    total = sum_refs[0][...]
    for ref in sum_refs[1:]:
        total = total + ref[...]
    inverse = lax.rsqrt(total[0:1] / WIDTH + epsilon)
    pull = inverse * inverse * inverse * total[1:2] / WIDTH
    return inverse, pull


def grad_kernel(n_sums, ids_ref, att_ref, q_ref, g_ref, gain_ref, *refs):
    sum_refs, (grad_ref, head_ref) = refs[:n_sums], refs[n_sums:]
    row, col = ids_of(ids_ref)
    first = wide(first_of(row, col))
    inverse, pull = scales(sum_refs)
    inverse, pull = column(inverse), column(pull)
    for h in range(q_ref.shape[1] // HD):
        c = head_cols(h)
        grad = (inverse * gain_ref[:, c] * g_ref[:, c].astype(f32) - pull * att_ref[:, c]).astype(bf16)
        grad_ref[:, c] = grad
        head_ref[h] = dot(q_ref[:, c] * first, grad, 0, 0).astype(bf16)


def back_kernel(n_sums, ids_ref, att_ref, q_ref, k_ref, v_ref, grad_ref, gain_ref, carry_ref, *refs):
    sum_refs, (normed_ref, gq_ref, gk_ref, gv_ref) = refs[:n_sums], refs[n_sums:]
    row, col = ids_of(ids_ref)
    first = wide(first_of(row, col))
    n = row.shape[1]
    inverse = column(scales(sum_refs)[0])
    t = lax.broadcasted_iota(jnp.int32, (n, n), 0)
    u = lax.broadcasted_iota(jnp.int32, (n, n), 1)
    same = (u <= t) & (col == row)
    same_t = (t <= u) & (col == row)
    for h in range(q_ref.shape[1] // HD):
        c = head_cols(h)
        q, k, v, grad = q_ref[:, c], k_ref[:, c], v_ref[:, c], grad_ref[:, c]
        normed_ref[:, c] = (att_ref[:, c] * inverse * gain_ref[:, c]).astype(bf16)
        gs = jnp.where(same, dot(grad, v, 1, 1), 0.0).astype(bf16)
        gq_ref[:, c] = (dot(gs, k, 1, 0) + dot(grad * first, carry_ref[h], 1, 1)).astype(bf16)
        gs_t = jnp.where(same_t, dot(v, grad, 1, 1), 0.0).astype(bf16)
        gk_ref[:, c] = dot(gs_t, q, 1, 0)
        w_t = jnp.where(same_t, dot(k, q, 1, 1), 0.0).astype(bf16)
        gv_ref[:, c] = dot(w_t, grad, 1, 0)


def last_kernel(ids_ref, k_ref, v_ref, gk_in, gv_in, back_ref, gk_ref, gv_ref):
    row, col = ids_of(ids_ref)
    last = wide(last_of(row, col))
    for h in range(k_ref.shape[1] // HD):
        c = head_cols(h)
        back = back_ref[h]
        gk_ref[:, c] = (gk_in[:, c] + dot(v_ref[:, c] * last, back, 1, 1)).astype(bf16)
        gv_ref[:, c] = (gv_in[:, c] + dot(k_ref[:, c] * last, back, 1, 0)).astype(bf16)


def call(kernel, outs, flops, *args):
    moved = sum(a.size * a.dtype.itemsize for a in (*args, *outs))
    return pl.pallas_call(
        kernel,
        out_shape=outs,
        cost_estimate=pl.CostEstimate(flops=flops, bytes_accessed=moved, transcendentals=0),
        compiler_params=pltpu.CompilerParams(vmem_limit_bytes=32 * 2**20),
    )(*args)


def spread(state, mask, groups):
    shape = state.shape
    pieces = state.reshape(groups, -1, shape[-1])
    here = lax.all_to_all(pieces, "seq", 0, 0)
    sums = jnp.einsum("cj,jmn->cmn", mask.astype(bf16), here, preferred_element_type=f32)
    return lax.all_to_all(sums.astype(bf16), "seq", 0, 0).reshape(shape)


def over_head(sums):
    size = lax.axis_size("head")
    power = size & (size - 1) == 0
    return [sums] + [
        lax.ppermute(sums, "head", [(i, i ^ k if power else (i + k) % size) for i in range(size)])
        for k in range(1, size)
    ]


def local(query_in, key_in, value_in, out_grad, norm_gain, doc_ids, start_group):
    n, cols = query_in.shape
    heads = cols // HD
    groups = lax.axis_size("seq")
    ids = doc_ids.reshape(1, n)
    gain = norm_gain.reshape(1, cols)
    group_ids = jnp.arange(groups, dtype=jnp.int32)
    state = jax.ShapeDtypeStruct((heads, HD, HD), bf16)
    tokens = jax.ShapeDtypeStruct((n, cols), bf16)
    tokens32 = jax.ShapeDtypeStruct((n, cols), f32)
    square = 2 * heads * n * n * HD
    narrow = 2 * heads * n * HD * HD

    (tail,) = call(tail_kernel, (state,), narrow, ids, key_in, value_in)
    before = (start_group[:, None] <= group_ids[None, :]) & (group_ids[None, :] < group_ids[:, None])
    carry = spread(tail, before, groups)
    (att_local,) = call(local_kernel, (tokens32,), 2 * square, ids, query_in, key_in, value_in)
    att, sums = call(
        attend_kernel,
        (tokens32, jax.ShapeDtypeStruct((2, n), f32)),
        narrow,
        ids, att_local, query_in, out_grad, gain, carry,
    )
    sums = over_head(sums)
    grad, head_state = call(
        functools.partial(grad_kernel, len(sums)),
        (tokens, state),
        narrow,
        ids, att, query_in, out_grad, gain, *sums,
    )
    after = (start_group[None, :] <= group_ids[:, None]) & (group_ids[:, None] < group_ids[None, :])
    back = spread(head_state, after, groups)
    normed, grad_query, gk, gv = call(
        functools.partial(back_kernel, len(sums)),
        (tokens, tokens, tokens32, tokens32),
        6 * square + narrow,
        ids, att, query_in, key_in, value_in, grad, gain, carry, *sums,
    )
    grad_key, grad_value = call(
        last_kernel, (tokens, tokens), 2 * narrow, ids, key_in, value_in, gk, gv, back
    )
    return normed, grad_query, grad_key, grad_value


def solution(mesh):
    block = P("seq", "head")
    return jax.shard_map(
        local,
        mesh=mesh,
        in_specs=(block, block, block, block, P("head"), P("seq"), P()),
        out_specs=(block, block, block, block),
        check_vma=False,
    )
```

time: 226 us -> 69.4 us (0.31)
  waiting for transfers between devices: 107 us -> 11.5 us
  other arithmetic: 25.3 us -> 0 us
  between operations: 16.9 us -> 0.8 us
  local copies, waits for them, and re-layouts: 22.8 us -> 9.74 us
  matrix products: 12.4 us -> 0.55 us
  loops' own time: 10.8 us -> 0 us
  starting transfers between devices: 0.08 us -> 9.09 us
  Pallas kernels: 0 us -> 8.05 us
    all_gather x2 -> x0, waiting for transfers between devices: 107 us -> none  [prefix(): everything = jax.tree.map(lambda part: lax.all_gather(part, axis), x)]
    all_to_all x0 -> x2, blocking collectives: none -> 29.1 us  [spread(): here = lax.all_to_all(pieces, 'seq', 0, 0)]
    unnamed x1 -> x0, blocking collectives: 23.6 us -> none
    select_n x16 -> x0, other arithmetic: 20.8 us -> none  [lap(): return jax.tree.map(lambda a, b: jnp.where(reached, a, b), new, before)]
    dot_general x12 -> x2, matrix products: 12.4 us -> 0.55 us  [spread(): jnp.einsum('cj,jmn->cmn', mask.astype(bf16), here, preferred_element_type...]
    another operation x2 -> x0, loops' own time: 10.8 us -> none  [prefix(): return lax.fori_loop(0, length, lap, start)]
    dynamic_slice x17 -> x0, local copies, waits for them, and re-layouts: 9.96 us -> none  [the longest x16 9.37 us: lap(): new = combine(before, jax.tree.map(lambda part: part[at], everything))]
    all_to_all x0 -> x2, waiting for transfers between devices: none -> 9.66 us  [spread(): return lax.all_to_all(sums.astype(bf16), 'seq', 0, 0).reshape(shape)]
  transfers between devices with their start and end apart: 2 -> 5, of which waited for: 2 -> 4; matrix products, arithmetic and copies ran while one was open for 6% -> 0% of each run, Pallas kernels for 0% -> 6%
where the time goes in v1:
time: 69.4 us; the launch traced here: 68.8 us
  blocking collectives  29.1 us (42%)
  waiting for transfers between devices  11.5 us (17%)
  local copies, waits for them, and re-layouts  9.74 us (14%)
  starting transfers between devices  9.09 us (13%)
  Pallas kernels  8.05 us (12%)
  between operations  0.8 us (1%)
    all_to_all x2, blocking collectives, spread(): here = lax.all_to_all(pieces, 'seq', 0, 0)  29.1 us
    all_to_all x2, waiting for transfers between devices, spread(): return lax.all_to_all(sums.astype(bf16), 'seq', 0, 0).reshape(shape)  9.66 us
    unnamed x34, local copies, waits for them, and re-layouts  8.25 us
    pallas_call x6, Pallas kernels, call(): pl.pallas_call(kernel, out_shape=outs, cost_estimate=pl.CostEstimate(flop...  8.05 us
    all_to_all x2, starting transfers between devices, spread(): return lax.all_to_all(sums.astype(bf16), 'seq', 0, 0).reshape(shape)  7.17 us
    ppermute x3, starting transfers between devices, over_head(): lax.ppermute(sums, 'head', [(i, i ^ k if power else (i + k) % size) for i...  1.92 us
    ppermute x3, waiting for transfers between devices, over_head(): lax.ppermute(sums, 'head', [(i, i ^ k if power else (i + k) % size) for i...  1.8 us
    dot_general x2, local copies, waits for them, and re-layouts, spread(): jnp.einsum('cj,jmn->cmn', mask.astype(bf16), here, preferred_element_type...  1.49 us
  transfers between devices with their start and end apart: 5, of which 4 were waited for; matrix products, arithmetic and copies ran while one was open for 0% of the time, Pallas kernels for 6%

profile of v1, /device:TPU:0, one launch (start us, length us, event | category | flops | bytes accessed | tf_op | source)
XLA Modules:
  0.0 68.8 jit_solution(2841602309121108593)
XLA Ops:
  0.6 0.7 copy-done.14
  1.3 1.0 %copy-done = bf16[256,1024]{1,0:T(8,128)(2,1)S(1)} copy-done((bf16[256,1024]{1,0:T(8,128)(2,1)S(1)}, bf16[256,1024]{1,0:T(8,128)(2,1)}, u32[]{:S(2)}) %copy-start) | copy-done | bytes 524312
  2.4 1.0 %copy-done.2 = bf16[256,1024]{1,0:T(8,128)(2,1)S(1)} copy-done((bf16[256,1024]{1,0:T(8,128)(2,1)S(1)}, bf16[256,1024]{1,0:T(8,128)(2,1)}, u32[]{:S(2)}) %copy-start.2) | copy-done | bytes 524312
  3.9 16.0 %all_to_all.20 = bf16[8,128,128]{2,1,0:T(8,128)(2,1)S(1)} all-to-all(bf16[8,128,128]{2,1,0:T(8,128)(2,1)S(1)} %shard_map.103), channel_id=1, replica_groups=mesh['seq'=8,'head'=4] {'seq'}, dimensions={0} | all-to-all | bytes 524288 | tf_op jit(solution)/shard_map/all_to_all | solution.py:158
  20.3 0.7 %copy.22 = bf16[8,128,128]{2,1,0:T(8,128)(2,1)} copy(bf16[8,128,128]{2,0,1:T(8,128)(2,1)S(1)} %fusion.2) | data formatting | bytes 524288 | tf_op jit(solution)/shard_map/cj,jmn->cmn/dot_general | solution.py:159
  21.0 3.6 %all-to-all-start.1 = ((bf16[8,128,128]{2,1,0:T(8,128)(2,1)}), bf16[8,128,128]{2,1,0:T(8,128)(2,1)S(1)}, u32[]{:S(2)}, u32[]{:S(2)}) async-start(bf16[8,128,128]{2,1,0:T(8,128)(2,1)} %copy.22), calls=%async_computation.1 | async-start | bytes 524288 | tf_op jit(solution)/shard_map/all_to_all | solution.py:160
  24.7 0.9 %shard_map.102.att_ref = f32[256,1024]{1,0:T(8,128)S(1)} custom-call(s32[1,256]{1,0:T(1,128)S(1)} %bitcast.9, bf16[256,1024]{1,0:T(8,128)(2,1)S(1)} %copy-done.4, bf16[256,1024]{1,0:T(8,128)(2,1)S(1)} %copy-done.1, bf16[256,1024]{1,0:T(8,128)(2,1)S(1)} %copy-done.3), custom_call_target="tpu_custom_call" | custom-call | flops 268435456 | bytes 2622464 | tf_op jit(solution)/shard_map/pallas_call | solution.py:147
  25.6 7.6 %all-to-all-done.1.carry_ref = bf16[8,128,128]{2,1,0:T(8,128)(2,1)S(1)} async-done(((bf16[8,128,128]{2,1,0:T(8,128)(2,1)}), bf16[8,128,128]{2,1,0:T(8,128)(2,1)S(1)}, u32[]{:S(2)}, u32[]{:S(2)}) %all-to-all-start.1) | async-done | bytes 262176 | tf_op jit(solution)/shard_map/all_to_all | solution.py:160
  33.2 0.7 shard_map.104
  34.0 1.6 %collective-permute-start.1 = (f32[2,256]{1,0:T(2,128)S(1)}, f32[2,256]{1,0:T(2,128)S(1)}, u32[]{:S(2)}, u32[]{:S(2)}) collective-permute-start(f32[2,256]{1,0:T(2,128)S(1)} %get-tuple-element.15.refs_0_), channel_id=1, source_target_pairs={{0,2},{1,3},{2,0},{3,1},{4,6},{5,7},{6,4},{7,5},{8,10},{9,11},{10,... | collective-permute-start | bytes 6152 | tf_op jit(solution)/shard_map/ppermute | solution.py:167
  35.8 1.1 %collective-permute-done.2.refs_3_ = f32[2,256]{1,0:T(2,128)S(1)} collective-permute-done((f32[2,256]{1,0:T(2,128)S(1)}, f32[2,256]{1,0:T(2,128)S(1)}, u32[]{:S(2)}, u32[]{:S(2)}) %collective-permute-start.2) | collective-permute-done | bytes 2080 | tf_op jit(solution)/shard_map/ppermute | solution.py:167
  36.9 0.7 collective-permute-done.1.refs_2_
  37.6 0.7 %shard_map.105 = (bf16[256,1024]{1,0:T(8,128)(2,1)S(1)}, bf16[8,128,128]{2,1,0:T(8,128)(2,1)S(1)}) custom-call(s32[1,256]{1,0:T(1,128)S(1)} %bitcast.11, f32[256,1024]{1,0:T(8,128)S(1)} %get-tuple-element.14.att_ref, bf16[256,1024]{1,0:T(8,128)(2,1)S(1)} %copy-done.4, bf16[256,1024]{1,0:T(8,128)(2,1)S(1)} %copy-done.7, f32[1,1024]{1,0:T(1,128)S(1)} %bitcast.15, ...), custom_call_target="tpu_custom_call" | custom-call | flops 67108864 | bytes 2896896 | tf_op jit(solution)/shard_map/pallas_call | solution.py:147
  38.4 13.1 %all_to_all.21 = bf16[8,128,128]{2,1,0:T(8,128)(2,1)S(1)} all-to-all(bf16[8,128,128]{2,1,0:T(8,128)(2,1)S(1)} %get-tuple-element.21), channel_id=1, replica_groups=mesh['seq'=8,'head'=4] {'seq'}, dimensions={0} | all-to-all | bytes 524288 | tf_op jit(solution)/shard_map/all_to_all | solution.py:158
  51.7 0.7 %copy.21 = bf16[8,128,128]{2,1,0:T(8,128)(2,1)} copy(bf16[8,128,128]{2,0,1:T(8,128)(2,1)S(1)} %fusion) | data formatting | bytes 524288 | tf_op jit(solution)/shard_map/cj,jmn->cmn/dot_general | solution.py:159
  52.5 3.6 %all-to-all-start.3 = ((bf16[8,128,128]{2,1,0:T(8,128)(2,1)}), bf16[8,128,128]{2,1,0:T(8,128)(2,1)S(1)}, u32[]{:S(2)}, u32[]{:S(2)}) async-start(bf16[8,128,128]{2,1,0:T(8,128)(2,1)} %copy.21), calls=%async_computation.3 | async-start | bytes 524288 | tf_op jit(solution)/shard_map/all_to_all | solution.py:160
  56.1 1.0 %copy-done.13 = bf16[256,1024]{1,0:T(8,128)(2,1)S(1)} copy-done((bf16[256,1024]{1,0:T(8,128)(2,1)S(1)}, bf16[256,1024]{1,0:T(8,128)(2,1)}, u32[]{:S(2)}) %copy-start.13) | copy-done | bytes 524312
  57.1 3.5 %shard_map.106 = (bf16[256,1024]{1,0:T(8,128)(2,1)}, bf16[256,1024]{1,0:T(8,128)(2,1)}, f32[256,1024]{1,0:T(8,128)S(1)}, f32[256,1024]{1,0:T(8,128)S(1)}) custom-call(s32[1,256]{1,0:T(1,128)S(1)} %bitcast.12, f32[256,1024]{1,0:T(8,128)S(1)} %copy-done.6, bf16[256,1024]{1,0:T(8,128)(2,1)S(1)} %copy-done.4, bf16[256,1024]{1,0:T(8,128)(2,1)S(1)} %copy-done.1, ...), custom_call_target="tpu_custom_call" | custom-call | flops 872415232 | bytes 6566912 | tf_op jit(solution)/shard_map/pallas_call | solution.py:147
  60.6 1.0 %copy-done.8 = f32[256,1024]{1,0:T(8,128)} copy-done((f32[256,1024]{1,0:T(8,128)}, f32[256,1024]{1,0:T(8,128)S(1)}, u32[]{:S(2)}) %copy-start.8) | copy-done | bytes 1048600
  61.6 0.9 %copy-done.10 = f32[256,1024]{1,0:T(8,128)} copy-done((f32[256,1024]{1,0:T(8,128)}, f32[256,1024]{1,0:T(8,128)S(1)}, u32[]{:S(2)}) %copy-start.10) | copy-done | bytes 1048600
  62.6 2.1 %all-to-all-done.3.back_ref = bf16[8,128,128]{2,1,0:T(8,128)(2,1)S(1)} async-done(((bf16[8,128,128]{2,1,0:T(8,128)(2,1)}), bf16[8,128,128]{2,1,0:T(8,128)(2,1)S(1)}, u32[]{:S(2)}, u32[]{:S(2)}) %all-to-all-start.3) | async-done | bytes 262176 | tf_op jit(solution)/shard_map/all_to_all | solution.py:160
  64.7 1.2 %copy-done.9 = f32[256,1024]{1,0:T(8,128)S(1)} copy-done((f32[256,1024]{1,0:T(8,128)S(1)}, f32[256,1024]{1,0:T(8,128)}, u32[]{:S(2)}) %copy-start.9) | copy-done | bytes 1048600
  65.9 1.2 %copy-done.11 = f32[256,1024]{1,0:T(8,128)S(1)} copy-done((f32[256,1024]{1,0:T(8,128)S(1)}, f32[256,1024]{1,0:T(8,128)}, u32[]{:S(2)}) %copy-start.11) | copy-done | bytes 1048600
  67.1 1.7 %shard_map.107 = (bf16[256,1024]{1,0:T(8,128)(2,1)}, bf16[256,1024]{1,0:T(8,128)(2,1)}) custom-call(s32[1,256]{1,0:T(1,128)S(1)} %bitcast.13, bf16[256,1024]{1,0:T(8,128)(2,1)S(1)} %copy-done.1, bf16[256,1024]{1,0:T(8,128)(2,1)S(1)} %copy-done.3, f32[256,1024]{1,0:T(8,128)S(1)} %copy-done.9, f32[256,1024]{1,0:T(8,128)S(1)} %copy-done.11, ...), custom_call_target="tpu_custom_call" | custom-call | flops 134217728 | bytes 4457472 | tf_op jit(solution)/shard_map/pallas_call | solution.py:147
  (32 shorter events, 1.5 us)
Async XLA Ops:
  0.6 0.7 copy-start.14
  1.3 1.0 %copy-start = (bf16[256,1024]{1,0:T(8,128)(2,1)S(1)}, bf16[256,1024]{1,0:T(8,128)(2,1)}, u32[]{:S(2)}) copy-start(bf16[256,1024]{1,0:T(8,128)(2,1)} %k_ref.7) | copy-start | bytes 1572868
  2.4 1.0 %copy-start.2 = (bf16[256,1024]{1,0:T(8,128)(2,1)S(1)}, bf16[256,1024]{1,0:T(8,128)(2,1)}, u32[]{:S(2)}) copy-start(bf16[256,1024]{1,0:T(8,128)(2,1)} %v_ref.7) | copy-start | bytes 1572868
  3.9 16.0 %copy-start.16 = (s32[8]{0:T(128)S(1)}, s32[8]{0:T(128)}, u32[]{:S(2)}) copy-start(s32[8]{0:T(128)} %param.13) | copy-start | bytes 100
  19.9 4.7 %copy-start.4 = (bf16[256,1024]{1,0:T(8,128)(2,1)S(1)}, bf16[256,1024]{1,0:T(8,128)(2,1)}, u32[]{:S(2)}) copy-start(bf16[256,1024]{1,0:T(8,128)(2,1)} %q_ref.7) | copy-start | bytes 1572868
  20.2 4.4 %copy-start.1 = (bf16[256,1024]{1,0:T(8,128)(2,1)S(1)}, bf16[256,1024]{1,0:T(8,128)(2,1)}, u32[]{:S(2)}) copy-start(bf16[256,1024]{1,0:T(8,128)(2,1)} %k_ref.7) | copy-start | bytes 1572868
  20.3 4.4 %copy-start.3 = (bf16[256,1024]{1,0:T(8,128)(2,1)S(1)}, bf16[256,1024]{1,0:T(8,128)(2,1)}, u32[]{:S(2)}) copy-start(bf16[256,1024]{1,0:T(8,128)(2,1)} %v_ref.7) | copy-start | bytes 1572868
  21.0 12.2 %all-to-all-start.1 = ((bf16[8,128,128]{2,1,0:T(8,128)(2,1)}), bf16[8,128,128]{2,1,0:T(8,128)(2,1)S(1)}, u32[]{:S(2)}, u32[]{:S(2)}) async-start(bf16[8,128,128]{2,1,0:T(8,128)(2,1)} %copy.22), calls=%async_computation.1 | async-start | bytes 524288 | tf_op jit(solution)/shard_map/all_to_all | solution.py:160
  24.6 8.5 %copy-start.7 = (bf16[256,1024]{1,0:T(8,128)(2,1)S(1)}, bf16[256,1024]{1,0:T(8,128)(2,1)}, u32[]{:S(2)}) copy-start(bf16[256,1024]{1,0:T(8,128)(2,1)} %g_ref.3) | copy-start | bytes 1572868
  24.6 8.5 %copy-start.15 = (f32[1024]{0:T(1024)S(1)}, f32[1024]{0:T(1024)}, u32[]{:S(2)}) copy-start(f32[1024]{0:T(1024)} %param.11) | copy-start | bytes 12292
  33.9 4.5 %copy-start.5 = (f32[256,1024]{1,0:T(8,128)}, f32[256,1024]{1,0:T(8,128)S(1)}, u32[]{:S(2)}) copy-start(f32[256,1024]{1,0:T(8,128)S(1)} %get-tuple-element.14.att_ref) | copy-start | bytes 3145732
  33.9 3.1 %collective-permute-start.2 = (f32[2,256]{1,0:T(2,128)S(1)}, f32[2,256]{1,0:T(2,128)S(1)}, u32[]{:S(2)}, u32[]{:S(2)}) collective-permute-start(f32[2,256]{1,0:T(2,128)S(1)} %get-tuple-element.15.refs_0_), channel_id=1, source_target_pairs={{0,3},{1,2},{2,1},{3,0},{4,7},{5,6},{6,5},{7,4},{8,11},{9,10},{10,... | collective-permute-start | bytes 6152 | tf_op jit(solution)/shard_map/ppermute | solution.py:167
  34.0 3.7 %collective-permute-start.1 = (f32[2,256]{1,0:T(2,128)S(1)}, f32[2,256]{1,0:T(2,128)S(1)}, u32[]{:S(2)}, u32[]{:S(2)}) collective-permute-start(f32[2,256]{1,0:T(2,128)S(1)} %get-tuple-element.15.refs_0_), channel_id=1, source_target_pairs={{0,2},{1,3},{2,0},{3,1},{4,6},{5,7},{6,4},{7,5},{8,10},{9,11},{10,... | collective-permute-start | bytes 6152 | tf_op jit(solution)/shard_map/ppermute | solution.py:167
  35.5 2.1 %collective-permute-start = (f32[2,256]{1,0:T(2,128)S(1)}, f32[2,256]{1,0:T(2,128)S(1)}, u32[]{:S(2)}, u32[]{:S(2)}) collective-permute-start(f32[2,256]{1,0:T(2,128)S(1)} %get-tuple-element.15.refs_0_), channel_id=1, source_target_pairs={{0,1},{1,0},{2,3},{3,2},{4,5},{5,4},{6,7},{7,6},{8,9},{9,8},{10,11... | collective-permute-start | bytes 6152 | tf_op jit(solution)/shard_map/ppermute | solution.py:167
  38.4 13.4 %copy-start.12 = (bf16[256,1024]{1,0:T(8,128)(2,1)}, bf16[256,1024]{1,0:T(8,128)(2,1)S(1)}, u32[]{:S(2)}) copy-start(bf16[256,1024]{1,0:T(8,128)(2,1)S(1)} %get-tuple-element.16.grad_ref) | copy-start | bytes 1572868
  38.4 17.7 %copy-start.6 = (f32[256,1024]{1,0:T(8,128)S(1)}, f32[256,1024]{1,0:T(8,128)}, u32[]{:S(2)}) copy-start(f32[256,1024]{1,0:T(8,128)} %copy-done.5) | copy-start | bytes 3145732
  52.5 12.2 %all-to-all-start.3 = ((bf16[8,128,128]{2,1,0:T(8,128)(2,1)}), bf16[8,128,128]{2,1,0:T(8,128)(2,1)S(1)}, u32[]{:S(2)}, u32[]{:S(2)}) async-start(bf16[8,128,128]{2,1,0:T(8,128)(2,1)} %copy.21), calls=%async_computation.3 | async-start | bytes 524288 | tf_op jit(solution)/shard_map/all_to_all | solution.py:160
  56.1 1.0 %copy-start.13 = (bf16[256,1024]{1,0:T(8,128)(2,1)S(1)}, bf16[256,1024]{1,0:T(8,128)(2,1)}, u32[]{:S(2)}) copy-start(bf16[256,1024]{1,0:T(8,128)(2,1)} %copy-done.12) | copy-start | bytes 1572868
  60.6 1.0 %copy-start.8 = (f32[256,1024]{1,0:T(8,128)}, f32[256,1024]{1,0:T(8,128)S(1)}, u32[]{:S(2)}) copy-start(f32[256,1024]{1,0:T(8,128)S(1)} %get-tuple-element.19.gk_in) | copy-start | bytes 3145732
  61.6 0.9 %copy-start.10 = (f32[256,1024]{1,0:T(8,128)}, f32[256,1024]{1,0:T(8,128)S(1)}, u32[]{:S(2)}) copy-start(f32[256,1024]{1,0:T(8,128)S(1)} %get-tuple-element.20.gv_in) | copy-start | bytes 3145732
  64.7 1.2 %copy-start.9 = (f32[256,1024]{1,0:T(8,128)S(1)}, f32[256,1024]{1,0:T(8,128)}, u32[]{:S(2)}) copy-start(f32[256,1024]{1,0:T(8,128)} %copy-done.8) | copy-start | bytes 3145732
  65.9 1.2 %copy-start.11 = (f32[256,1024]{1,0:T(8,128)S(1)}, f32[256,1024]{1,0:T(8,128)}, u32[]{:S(2)}) copy-start(f32[256,1024]{1,0:T(8,128)} %copy-done.10) | copy-start | bytes 3145732

commit v2 on v1

v2 whole, which is shorter than its diff:
```python
import functools

import jax
import jax.numpy as jnp
from jax import lax
from jax.experimental import pallas as pl
from jax.experimental.pallas import tpu as pltpu
from jax.sharding import PartitionSpec as P

H = 32
HD = 128
WIDTH = H * HD

epsilon = 1e-06

ONE, TWO, PAIRS, ANY = range(4)

f32 = jnp.float32
bf16 = jnp.bfloat16


def dot(a, b, da, db):
    return lax.dot_general(a, b, (((da,), (db,)), ((), ())), preferred_element_type=f32)


def head_cols(h):
    return slice(h * HD, (h + 1) * HD)


def column(row):
    n = row.shape[1]
    at = lax.broadcasted_iota(jnp.int32, (n, n), 0) == lax.broadcasted_iota(jnp.int32, (n, n), 1)
    return jnp.sum(jnp.where(at, row, 0.0), axis=1, keepdims=True)


def as_row(col):
    n = col.shape[0]
    at = lax.broadcasted_iota(jnp.int32, (n, n), 0) == lax.broadcasted_iota(jnp.int32, (n, n), 1)
    return jnp.sum(jnp.where(at, col, 0.0), axis=0, keepdims=True)


def ids_of(ids_ref):
    row = ids_ref[...].astype(f32)
    return row, column(row)


def wide(col, dtype=bf16):
    return jnp.broadcast_to(col, (col.shape[0], HD)).astype(dtype)


def tail_kernel(
    start_hbm, ids_hbm, k_hbm, v_hbm,
    tail_ref, tail2_ref, first_ref, last_ref, needs_ref, plan_ref,
    start_ref, ids_ref, k_ref, v_ref, sems,
):
    chunks = k_ref.shape[0]
    cols = k_ref.shape[2]
    small = [
        pltpu.make_async_copy(ids_hbm, ids_ref, sems.at[2 * chunks]),
        pltpu.make_async_copy(start_hbm, start_ref, sems.at[2 * chunks + 1]),
    ]
    large = []
    for i in range(chunks):
        at = pl.ds(i * cols, cols)
        large.append((
            pltpu.make_async_copy(k_hbm.at[:, at], k_ref.at[i], sems.at[2 * i]),
            pltpu.make_async_copy(v_hbm.at[:, at], v_ref.at[i], sems.at[2 * i + 1]),
        ))
    for copy in small:
        copy.start()
    for pair in large:
        for copy in pair:
            copy.start()
    for copy in small:
        copy.wait()
    me, top = lax.axis_index("seq"), start_ref.shape[0] - 1
    blocks, pairs = jnp.int32(0), jnp.int32(0)
    for c in range(top + 1):
        begin = start_ref[c]
        blocks = jnp.maximum(blocks, c - begin)
        pairs = jnp.maximum(pairs, c // 2 - (begin >> 1))
    plan_ref[0] = jnp.where(blocks <= 2, jnp.maximum(blocks - 1, 0), jnp.where(pairs <= 1, PAIRS, ANY))
    for step in (1, 2):
        needs_ref[step - 1 : step, :] = jnp.full((1, HD), jnp.where(start_ref[me] <= me - step, 1.0, 0.0), f32)
    need, need2 = [
        (me + step <= top) & (start_ref[jnp.minimum(me + step, top)] <= me) for step in (1, 2)
    ]
    row, col = ids_of(ids_ref)
    first_ref[...] = wide((col == row[:, :1]).astype(f32))
    last = (col == row[:, -1:]).astype(f32)
    last_ref[...] = wide(last)
    last = wide(last * jnp.where(need, 1.0, 0.0))
    for i, pair in enumerate(large):
        for copy in pair:
            copy.wait()
        for j in range(cols // HD):
            state = dot(k_ref[i, :, head_cols(j)] * last, v_ref[i, :, head_cols(j)], 0, 0)
            h = i * (cols // HD) + j
            tail_ref[h] = state.astype(bf16)
            tail2_ref[h] = jnp.where(need2, state, 0.0).astype(bf16)


def local_kernel(ids_ref, first_ref, q_ref, k_ref, v_ref, *refs):
    far_refs, att_ref = refs[:-1], refs[-1]
    row, col = ids_of(ids_ref)
    n = row.shape[1]
    t = lax.broadcasted_iota(jnp.int32, (n, n), 0)
    u = lax.broadcasted_iota(jnp.int32, (n, n), 1)
    same = (u <= t) & (col == row)
    for h in range(q_ref.shape[1] // HD):
        c = head_cols(h)
        w = jnp.where(same, dot(q_ref[:, c], k_ref[:, c], 1, 1), 0.0).astype(bf16)
        att = dot(w, v_ref[:, c], 1, 0)
        for far_ref in far_refs:
            att = att + dot(q_ref[:, c] * first_ref[...], far_ref[h], 1, 0)
        att_ref[:, c] = att


def joined(plan, way, refs, h):
    if plan != PAIRS:
        return refs[0][h] if len(refs) == 1 else refs[0][h] + refs[1][h]
    start_ref, twin_ref, inner_ref, outer_ref = refs
    me, top = lax.axis_index("seq"), start_ref.shape[0] - 1
    pair, odd = me >> 1, me & 1
    if way == 1:
        twin = (odd == 1) & (start_ref[me] < me)
        far = start_ref[me] < 2 * pair
    else:
        twin = (odd == 0) & (start_ref[jnp.minimum(me + 1, top)] <= me)
        beyond = 2 * pair + 2
        far = (beyond <= top) & (start_ref[jnp.minimum(beyond, top)] <= me)
    inner = (pair & 1 == 1) == (way == 1)
    zero = jnp.zeros(twin_ref.shape[1:], bf16)
    from_pair = jnp.where(inner, inner_ref[h], outer_ref[h])
    return jnp.where(twin, twin_ref[h], zero) + jnp.where(far, from_pair, zero)


def pair_kernel(way, start_ref, own_ref, twin_ref, out_ref):
    me, top = lax.axis_index("seq"), start_ref.shape[0] - 1
    pair, odd = me >> 1, me & 1
    if way == 1:
        both = start_ref[jnp.minimum(2 * pair + 2, top)] <= 2 * pair
    else:
        both = start_ref[jnp.minimum(2 * pair + 1, top)] < 2 * pair
    own_near = (odd == 1) == (way == 1)
    zero = jnp.zeros(own_ref.shape[1:], bf16)
    for h in range(own_ref.shape[0]):
        own = jnp.where(own_near | both, own_ref[h], zero)
        twin = jnp.where(both | jnp.logical_not(own_near), twin_ref[h], zero)
        out_ref[h] = own + twin


def attend_kernel(plan, first_ref, att_ref, q_ref, g_ref, gain_ref, *refs):
    state_refs, (out_ref, sums_ref) = refs[:-2], refs[-2:]
    first = first_ref[...]
    square = jnp.zeros(first.shape, f32)
    cross = jnp.zeros(first.shape, f32)
    for h in range(q_ref.shape[1] // HD):
        c = head_cols(h)
        att = att_ref[:, c] + dot(q_ref[:, c] * first, joined(plan, 1, state_refs, h), 1, 0)
        out_ref[:, c] = att
        square = square + att * att
        cross = cross + gain_ref[:, c] * g_ref[:, c].astype(f32) * att
    sums_ref[0:1, :] = as_row(jnp.sum(square, axis=1, keepdims=True))
    sums_ref[1:2, :] = as_row(jnp.sum(cross, axis=1, keepdims=True))


def scales(sum_refs):
    total = sum_refs[0][...]
    for ref in sum_refs[1:]:
        total = total + ref[...]
    inverse = lax.rsqrt(total[0:1] / WIDTH + epsilon)
    pull = inverse * inverse * inverse * total[1:2] / WIDTH
    return inverse, pull


def grad_kernel(n_heads, needs_ref, first_ref, att_ref, q_ref, g_ref, gain_ref, *refs):
    sum_refs, grad_ref, head_refs = refs[: -n_heads - 1], refs[-n_heads - 1], refs[-n_heads:]
    first = first_ref[...]
    needs = [jnp.broadcast_to(needs_ref[i : i + 1, :], (HD, HD)) > 0.5 for i in range(n_heads)]
    inverse, pull = scales(sum_refs)
    inverse, pull = column(inverse), column(pull)
    for h in range(q_ref.shape[1] // HD):
        c = head_cols(h)
        grad = (inverse * gain_ref[:, c] * g_ref[:, c].astype(f32) - pull * att_ref[:, c]).astype(bf16)
        grad_ref[:, c] = grad
        state = dot(q_ref[:, c] * first, grad, 0, 0)
        for ref, need in zip(head_refs, needs):
            ref[h] = jnp.where(need, state, 0.0).astype(bf16)


def back_kernel(plan, n_sums, n_far, ids_ref, first_ref, last_ref, att_ref, q_ref, k_ref, v_ref, grad_ref, gain_ref, *refs):
    sum_refs, refs, (normed_ref, gq_ref, gk_ref, gv_ref) = refs[:n_sums], refs[n_sums:-4], refs[-4:]
    far_refs, state_refs = refs[:n_far], refs[n_far:]
    inverse = column(scales(sum_refs)[0])
    row, col = ids_of(ids_ref)
    first = first_ref[...]
    n = row.shape[1]
    t = lax.broadcasted_iota(jnp.int32, (n, n), 0)
    u = lax.broadcasted_iota(jnp.int32, (n, n), 1)
    same = (u <= t) & (col == row)
    same_t = (t <= u) & (col == row)
    for h in range(q_ref.shape[1] // HD):
        c = head_cols(h)
        q, k, v, grad = q_ref[:, c], k_ref[:, c], v_ref[:, c], grad_ref[:, c]
        normed_ref[:, c] = (att_ref[:, c] * inverse * gain_ref[:, c]).astype(bf16)
        gs = jnp.where(same, dot(grad, v, 1, 1), 0.0).astype(bf16)
        gq_ref[:, c] = (dot(gs, k, 1, 0) + dot(grad * first, joined(plan, 1, state_refs, h), 1, 1)).astype(bf16)
        gs_t = jnp.where(same_t, dot(v, grad, 1, 1), 0.0).astype(bf16)
        gk = dot(gs_t, q, 1, 0)
        w_t = jnp.where(same_t, dot(k, q, 1, 1), 0.0).astype(bf16)
        gv = dot(w_t, grad, 1, 0)
        for far_ref in far_refs:
            gk = gk + dot(v * last_ref[...], far_ref[h], 1, 1)
            gv = gv + dot(k * last_ref[...], far_ref[h], 1, 0)
        gk_ref[:, c] = gk
        gv_ref[:, c] = gv


def last_kernel(plan, last_ref, k_ref, v_ref, gk_in, gv_in, *refs):
    state_refs, (gk_hbm, gv_hbm, gk_ref, gv_ref, sems) = refs[:-5], refs[-5:]
    last = last_ref[...]
    chunks, _, cols = gk_ref.shape
    copies = []
    for i in range(chunks):
        for j in range(cols // HD):
            h = i * (cols // HD) + j
            c = head_cols(h)
            back = joined(plan, -1, state_refs, h)
            gk_ref[i, :, head_cols(j)] = (gk_in[:, c] + dot(v_ref[:, c] * last, back, 1, 1)).astype(bf16)
            gv_ref[i, :, head_cols(j)] = (gv_in[:, c] + dot(k_ref[:, c] * last, back, 1, 0)).astype(bf16)
        at = pl.ds(i * cols, cols)
        copies.append(pltpu.make_async_copy(gk_ref.at[i], gk_hbm.at[:, at], sems.at[2 * i]))
        copies.append(pltpu.make_async_copy(gv_ref.at[i], gv_hbm.at[:, at], sems.at[2 * i + 1]))
        copies[-2].start()
        copies[-1].start()
    for copy in copies:
        copy.wait()


def shape_of(a):
    return jax.ShapeDtypeStruct(a.shape, a.dtype)


def call(kernel, outs, flops, *args, in_space=None, out_space=None, scratch=()):
    moved = sum(a.size * a.dtype.itemsize for a in (*args, *outs))

    def spec(a, space):
        return pl.BlockSpec(memory_space=space or (pltpu.SMEM if len(a.shape) == 1 else pltpu.VMEM))

    return pl.pallas_call(
        kernel,
        out_shape=outs,
        in_specs=[spec(a, in_space) for a in args],
        out_specs=tuple(spec(a, out_space) for a in outs),
        scratch_shapes=scratch,
        cost_estimate=pl.CostEstimate(flops=flops, bytes_accessed=moved, transcendentals=0),
        compiler_params=pltpu.CompilerParams(vmem_limit_bytes=32 * 2**20),
    )(*args)


def spread(state, mask, groups):
    shape = state.shape
    pieces = state.reshape(groups, -1, shape[-1])
    here = lax.all_to_all(pieces, "seq", 0, 0)
    sums = jnp.einsum("cj,jmn->cmn", mask.astype(bf16), here, preferred_element_type=f32)
    return lax.all_to_all(sums.astype(bf16), "seq", 0, 0).reshape(shape)


def over_head(sums):
    size = lax.axis_size("head")
    power = size & (size - 1) == 0
    return [sums] + [
        lax.ppermute(sums, "head", [(i, i ^ k if power else (i + k) % size) for i in range(size)])
        for k in range(1, size)
    ]


def exchange(plan, way, states, start_group):
    groups = lax.axis_size("seq")
    if plan in (ONE, TWO):
        return [
            lax.ppermute(state, "seq", [(i, i + way * k) for i in range(groups) if 0 <= i + way * k < groups])
            for k, state in enumerate(states, 1)
        ]
    (state,) = states
    if plan == PAIRS:
        twin = lax.ppermute(state, "seq", [(i, i ^ 1) for i in range(groups)])
        (both,) = call(functools.partial(pair_kernel, way), (shape_of(state),), 0, start_group, state, twin)
        ends = (0, 1, groups - 2, groups - 1)
        outer = [i ^ 1 if i in ends else ((i - 2) ^ 2) + 2 for i in range(groups)]
        return [
            start_group,
            twin,
            lax.ppermute(both, "seq", [(i, i ^ 2) for i in range(groups)]),
            lax.ppermute(both, "seq", list(enumerate(outer))),
        ]
    ids = jnp.arange(groups, dtype=jnp.int32)
    reach = (start_group[:, None] <= ids[None, :]) & (ids[None, :] < ids[:, None])
    return [spread(state, reach if way == 1 else reach.T, groups)]


def layer(plan, tail, tail2, first, last, needs, query_in, key_in, value_in, out_grad, gain, ids, start_group):
    n, cols = query_in.shape
    heads = cols // HD
    tokens = shape_of(query_in)
    tokens32 = jax.ShapeDtypeStruct((n, cols), f32)
    square = 2 * heads * n * n * HD
    narrow = 2 * heads * n * HD * HD

    earlier = exchange(plan, 1, [tail, tail2] if plan == TWO else [tail], start_group)
    near, far = (earlier[:1], earlier[1:]) if plan == TWO else (earlier, [])
    (att_local,) = call(local_kernel, (tokens32,), 2 * square, ids, first, query_in, key_in, value_in, *far)
    att, sums = call(
        functools.partial(attend_kernel, plan),
        (tokens32, jax.ShapeDtypeStruct((2, n), f32)),
        narrow,
        first, att_local, query_in, out_grad, gain, *near,
    )
    sums = over_head(sums)
    n_heads = 2 if plan == TWO else 1
    grad, *head_states = call(
        functools.partial(grad_kernel, n_heads),
        (tokens, *[shape_of(tail)] * n_heads),
        narrow,
        needs, first, att, query_in, out_grad, gain, *sums,
    )
    later = exchange(plan, -1, head_states, start_group)
    near, far = (later[:1], later[1:]) if plan == TWO else (later, [])
    normed, grad_query, gk, gv = call(
        functools.partial(back_kernel, plan, len(sums), len(far)),
        (tokens, tokens, tokens32, tokens32),
        6 * square + narrow,
        ids, first, last, att, query_in, key_in, value_in, grad, gain, *sums, *far, *earlier,
    )
    chunks = 4 if heads % 4 == 0 else 1
    part = pltpu.VMEM((chunks, n, cols // chunks), bf16)
    grad_key, grad_value = call(
        functools.partial(last_kernel, plan),
        (tokens, tokens),
        2 * narrow,
        last, key_in, value_in, gk, gv, *near,
        out_space=pltpu.HBM,
        scratch=[part, part, pltpu.SemaphoreType.DMA((2 * chunks,))],
    )
    return normed, grad_query, grad_key, grad_value


def local(query_in, key_in, value_in, out_grad, norm_gain, doc_ids, start_group):
    n, cols = query_in.shape
    heads = cols // HD
    ids, gain = doc_ids.reshape(1, n), norm_gain.reshape(1, cols)
    state = jax.ShapeDtypeStruct((heads, HD, HD), bf16)
    mask = jax.ShapeDtypeStruct((n, HD), bf16)
    chunks = 4 if heads % 4 == 0 else 1
    part = pltpu.VMEM((chunks, n, cols // chunks), bf16)
    *held, plan = call(
        tail_kernel,
        (
            state, state, mask, mask,
            jax.ShapeDtypeStruct((2, HD), f32), jax.ShapeDtypeStruct((1,), jnp.int32),
        ),
        2 * heads * n * HD * HD,
        start_group, ids, key_in, value_in,
        in_space=pltpu.HBM,
        scratch=[
            pltpu.SMEM(start_group.shape, jnp.int32),
            pltpu.VMEM((1, n), jnp.int32),
            part, part,
            pltpu.SemaphoreType.DMA((2 * chunks + 2,)),
        ],
    )
    plans = (ONE, TWO, PAIRS if start_group.shape[0] % 4 == 0 else ANY, ANY)
    return lax.switch(
        plan[0],
        [functools.partial(layer, way) for way in plans],
        *held, query_in, key_in, value_in, out_grad, gain, ids, start_group,
    )


def solution(mesh):
    block = P("seq", "head")
    return jax.shard_map(
        local,
        mesh=mesh,
        in_specs=(block, block, block, block, P("head"), P("seq"), P()),
        out_specs=(block, block, block, block),
        check_vma=False,
    )
```

time: 69.4 us -> 45.1 us (0.65)
  blocking collectives: 29.1 us -> 0 us
  local copies, waits for them, and re-layouts: 9.74 us -> 1.36 us
  waiting for transfers between devices: 11.5 us -> 18 us
  starting transfers between devices: 9.09 us -> 12.9 us
  Pallas kernels: 8.05 us -> 10.5 us
  between operations: 0.8 us -> 1.51 us
    all_to_all x2 -> x0, blocking collectives: 29.1 us -> none  [spread(): here = lax.all_to_all(pieces, 'seq', 0, 0)]
    ppermute x0 -> x4, waiting for transfers between devices: none -> 15.3 us  [exchange(): lax.ppermute(state, 'seq', [(i, i + way * k) for i in range(groups) if 0...]
    ppermute x0 -> x4, starting transfers between devices: none -> 11 us  [exchange(): lax.ppermute(state, 'seq', [(i, i + way * k) for i in range(groups) if 0...]
    all_to_all x2 -> x0, waiting for transfers between devices: 9.66 us -> none  [spread(): return lax.all_to_all(sums.astype(bf16), 'seq', 0, 0).reshape(shape)]
    all_to_all x2 -> x0, starting transfers between devices: 7.17 us -> none  [spread(): return lax.all_to_all(sums.astype(bf16), 'seq', 0, 0).reshape(shape)]
    unnamed x34 -> x10, local copies, waits for them, and re-layouts: 8.25 us -> 1.35 us
    pallas_call x6, Pallas kernels: 8.05 us -> 10.5 us  [call(): pl.pallas_call(kernel, out_shape=outs, in_specs=[spec(a, in_space) for a...]
    dot_general x2 -> x0, local copies, waits for them, and re-layouts: 1.49 us -> none  [spread(): jnp.einsum('cj,jmn->cmn', mask.astype(bf16), here, preferred_element_type...]
  transfers between devices with their start and end apart: 5 -> 7, of which waited for: 4 -> 5; matrix products, arithmetic and copies ran while one was open for 0% -> 0% of each run, Pallas kernels for 6% -> 13%
where the time goes in v2:
time: 45.1 us; the launch traced here: 44.5 us
  waiting for transfers between devices  18 us (40%)
  starting transfers between devices  12.9 us (29%)
  Pallas kernels  10.5 us (23%)
  between operations  1.51 us (3%)
  local copies, waits for them, and re-layouts  1.36 us (3%)
    ppermute x4, waiting for transfers between devices, exchange(): lax.ppermute(state, 'seq', [(i, i + way * k) for i in range(groups) if 0...  15.3 us
    ppermute x4, starting transfers between devices, exchange(): lax.ppermute(state, 'seq', [(i, i + way * k) for i in range(groups) if 0...  11 us
    pallas_call x6, Pallas kernels, call(): pl.pallas_call(kernel, out_shape=outs, in_specs=[spec(a, in_space) for a...  10.5 us
    ppermute x3, waiting for transfers between devices, over_head(): lax.ppermute(sums, 'head', [(i, i ^ k if power else (i + k) % size) for i...  2.7 us
    ppermute x3, starting transfers between devices, over_head(): lax.ppermute(sums, 'head', [(i, i ^ k if power else (i + k) % size) for i...  1.93 us
    unnamed x10, local copies, waits for them, and re-layouts  1.35 us
  transfers between devices with their start and end apart: 7, of which 5 were waited for; matrix products, arithmetic and copies ran while one was open for 0% of the time, Pallas kernels for 13%

profile of v2, /device:TPU:0, one launch (start us, length us, event | category | flops | bytes accessed | tf_op | source)
XLA Modules:
  0.0 44.5 jit_solution(17344926793334974452)
XLA Ops:
  0.7 0.6 %copy-done.19 = s32[8]{0:T(128)S(1)} copy-done((s32[8]{0:T(128)S(1)}, s32[8]{0:T(128)}, u32[]{:S(2)}) %copy-start.19) | copy-done | bytes 56
  1.3 0.0 copy-done.16
  1.3 2.4 %shard_map.102 = (bf16[8,128,128]{2,1,0:T(8,128)(2,1)S(1)}, bf16[8,128,128]{2,1,0:T(8,128)(2,1)S(1)}, bf16[256,128]{1,0:T(8,128)(2,1)S(1)}, bf16[256,128]{1,0:T(...) custom-call(s32[8]{0:T(128)S(1)} %copy-done.19, s32[1,256]{1,0:T(1,128)S(1)} %bitcast.12, bf16[256,1024]{1,0:T(8,128)(2,1)} %k_hbm.1, ...), custom_call_target="tpu_custom_call" | custom-call | flops 67108864 | bytes 1706020 | tf_op jit(solution)/shard_map/pallas_call | solution.py:251
  4.4 0.0 copy-start.14
  4.4 0.7 %copy-done.14 = f32[1024]{0:T(1024)S(1)} copy-done((f32[1024]{0:T(1024)S(1)}, f32[1024]{0:T(1024)}, u32[]{:S(2)}) %copy-start.14) | copy-done | bytes 4120
  5.1 39.3 %conditional.1 = (bf16[256,1024]{1,0:T(8,128)(2,1)}, bf16[256,1024]{1,0:T(8,128)(2,1)}, bf16[256,1024]{1,0:T(8,128)(2,1)}, bf16[256,1024]{1,0:T(8,128)(2,1)}) conditional(s32[]{:T(128)} %bitcast.3, (s32[1,256]{1,0:T(1,128)S(1)}, bf16[256,128]{1,0:T(8,128)(2,1)S(1)}, bf16[256,1024]{1,0:T(8,128)(2,1)S(1)}, ...), branch_computations={%region_0.0_spmd, %region_1.0_spmd, %region_2.0_spmd, %region_3.0_... | conditional | flops 1413480960 | bytes 37709388 | solution.py:374
  5.1 4.9 %collective-permute-start.5 = (bf16[8,128,128]{2,1,0:T(8,128)(2,1)S(1)}, bf16[8,128,128]{2,1,0:T(8,128)(2,1)S(1)}, u32[]{:S(2)}, u32[]{:S(2)}) collective-permute-start(bf16[8,128,128]{2,1,0:T(8,128)(2,1)S(1)} %get-tuple-element.112), channel_id=1, source_target_pairs={{0,8},{4,12},{8,16},{12,20},{16,24},{20,28},{1,9},{5,13},{9,17},{1... | collective-permute-start | bytes 786440 | tf_op jit(solution)/shard_map/cond/branch_1_fun/ppermute | solution.py:283
  10.0 3.4 %collective-permute-start.6 = (bf16[8,128,128]{2,1,0:T(8,128)(2,1)S(1)}, bf16[8,128,128]{2,1,0:T(8,128)(2,1)S(1)}, u32[]{:S(2)}, u32[]{:S(2)}) collective-permute-start(bf16[8,128,128]{2,1,0:T(8,128)(2,1)S(1)} %get-tuple-element.115), channel_id=1, source_target_pairs={{0,4},{4,8},{8,12},{12,16},{16,20},{20,24},{24,28},{1,5},{5,9},{9,... | collective-permute-start | bytes 786440 | tf_op jit(solution)/shard_map/cond/branch_1_fun/ppermute | solution.py:283
  13.4 2.1 %collective-permute-done.5.refs_0_.refs_6_ = bf16[8,128,128]{2,1,0:T(8,128)(2,1)S(1)} collective-permute-done((bf16[8,128,128]{2,1,0:T(8,128)(2,1)S(1)}, bf16[8,128,128]{2,1,0:T(8,128)(2,1)S(1)}, u32[]{:S(2)}, u32[]{:S(2)}) %collective-permute-start.5) | collective-permute-done | bytes 262176 | tf_op jit(solution)/shard_map/cond/branch_1_fun/ppermute | solution.py:283
  15.5 2.2 %branch_1_fun.5.att_ref = f32[256,1024]{1,0:T(8,128)S(1)} custom-call(s32[1,256]{1,0:T(1,128)S(1)} %get-tuple-element.106.ids_ref, bf16[256,128]{1,0:T(8,128)(2,1)S(1)} %get-tuple-element.107.first_ref, bf16[256,1024]{1,0:T(8,128)(2,1)S(1)} %get-tuple-element.109.q_ref, bf16[256,1024]{1,0:T(8,128)(2,1)S(1)} %get-tuple-element.110.k_ref, ...), custom_call_target="tpu_custom_call" | custom-call | flops 268435456 | bytes 2950144 | tf_op jit(solution)/shard_map/cond/branch_1_fun/pallas_call | solution.py:251
  17.8 0.9 %collective-permute-done.6.refs_0_.refs_5_ = bf16[8,128,128]{2,1,0:T(8,128)(2,1)S(1)} collective-permute-done((bf16[8,128,128]{2,1,0:T(8,128)(2,1)S(1)}, bf16[8,128,128]{2,1,0:T(8,128)(2,1)S(1)}, u32[]{:S(2)}, u32[]{:S(2)}) %collective-permute-start.6) | collective-permute-done | bytes 262176 | tf_op jit(solution)/shard_map/cond/branch_1_fun/ppermute | solution.py:283
  18.7 0.5 %branch_1_fun.6 = (f32[256,1024]{1,0:T(8,128)S(1)}, f32[2,256]{1,0:T(2,128)S(1)}) custom-call(bf16[256,128]{1,0:T(8,128)(2,1)S(1)} %get-tuple-element.107.first_ref, f32[256,1024]{1,0:T(8,128)S(1)} %branch_1_fun.5.att_ref, bf16[256,1024]{1,0:T(8,128)(2,1)S(1)} %get-tuple-element.109.q_ref, bf16[256,1024]{1,0:T(8,128)(2,1)S(1)} %copy-done.11, ...), custom_call_target="tpu_custom_call" | custom-call | flops 67108864 | bytes 3479552 | tf_op jit(solution)/shard_map/cond/branch_1_fun/pallas_call | solution.py:251
  19.2 0.1 collective-permute-start.7
  19.3 1.6 %collective-permute-start.8 = (f32[2,256]{1,0:T(2,128)S(1)}, f32[2,256]{1,0:T(2,128)S(1)}, u32[]{:S(2)}, u32[]{:S(2)}) collective-permute-start(f32[2,256]{1,0:T(2,128)S(1)} %get-tuple-element.118.refs_0_), channel_id=1, source_target_pairs={{0,2},{1,3},{2,0},{3,1},{4,6},{5,7},{6,4},{7,5},{8,10},{9,11},{10,... | collective-permute-start | bytes 6152 | tf_op jit(solution)/shard_map/cond/branch_1_fun/ppermute | solution.py:274
  20.9 0.3 collective-permute-start.9
  21.2 0.0 collective-permute-done.7.refs_1_
  21.2 1.8 %collective-permute-done.8.refs_2_ = f32[2,256]{1,0:T(2,128)S(1)} collective-permute-done((f32[2,256]{1,0:T(2,128)S(1)}, f32[2,256]{1,0:T(2,128)S(1)}, u32[]{:S(2)}, u32[]{:S(2)}) %collective-permute-start.8) | collective-permute-done | bytes 2080 | tf_op jit(solution)/shard_map/cond/branch_1_fun/ppermute | solution.py:274
  23.0 0.9 %collective-permute-done.9.refs_3_ = f32[2,256]{1,0:T(2,128)S(1)} collective-permute-done((f32[2,256]{1,0:T(2,128)S(1)}, f32[2,256]{1,0:T(2,128)S(1)}, u32[]{:S(2)}, u32[]{:S(2)}) %collective-permute-start.9) | collective-permute-done | bytes 2080 | tf_op jit(solution)/shard_map/cond/branch_1_fun/ppermute | solution.py:274
  23.9 0.6 %branch_1_fun.7 = (bf16[256,1024]{1,0:T(8,128)(2,1)S(1)}, bf16[8,128,128]{2,1,0:T(8,128)(2,1)S(1)}, bf16[8,128,128]{2,1,0:T(8,128)(2,1)S(1)}) custom-call(f32[2,128]{1,0:T(2,128)S(1)} %get-tuple-element.117.needs_ref, bf16[256,128]{1,0:T(8,128)(2,1)S(1)} %get-tuple-element.107.first_ref, f32[256,1024]{1,0:T(8,128)S(1)} %get-tuple-element.116.att_ref, ...), custom_call_target="tpu_custom_call" | custom-call | flops 67108864 | bytes 3224576 | tf_op jit(solution)/shard_map/cond/branch_1_fun/pallas_call | solution.py:251
  24.5 1.3 %collective-permute-start.10 = (bf16[8,128,128]{2,1,0:T(8,128)(2,1)S(1)}, bf16[8,128,128]{2,1,0:T(8,128)(2,1)S(1)}, u32[]{:S(2)}, u32[]{:S(2)}) collective-permute-start(bf16[8,128,128]{2,1,0:T(8,128)(2,1)S(1)} %get-tuple-element.120), channel_id=1, source_target_pairs={{8,0},{12,4},{16,8},{20,12},{24,16},{28,20},{9,1},{13,5},{17,9},{2... | collective-permute-start | bytes 786440 | tf_op jit(solution)/shard_map/cond/branch_1_fun/ppermute | solution.py:283
  25.8 1.3 %collective-permute-start.11 = (bf16[8,128,128]{2,1,0:T(8,128)(2,1)S(1)}, bf16[8,128,128]{2,1,0:T(8,128)(2,1)S(1)}, u32[]{:S(2)}, u32[]{:S(2)}) collective-permute-start(bf16[8,128,128]{2,1,0:T(8,128)(2,1)S(1)} %get-tuple-element.125), channel_id=1, source_target_pairs={{4,0},{8,4},{12,8},{16,12},{20,16},{24,20},{28,24},{5,1},{9,5},{13... | collective-permute-start | bytes 786440 | tf_op jit(solution)/shard_map/cond/branch_1_fun/ppermute | solution.py:283
  27.1 12.3 %collective-permute-done.10.refs_4_ = bf16[8,128,128]{2,1,0:T(8,128)(2,1)S(1)} collective-permute-done((bf16[8,128,128]{2,1,0:T(8,128)(2,1)S(1)}, bf16[8,128,128]{2,1,0:T(8,128)(2,1)S(1)}, u32[]{:S(2)}, u32[]{:S(2)}) %collective-permute-start.10) | collective-permute-done | bytes 262176 | tf_op jit(solution)/shard_map/cond/branch_1_fun/ppermute | solution.py:283
  39.3 3.5 %branch_1_fun.8 = (bf16[256,1024]{1,0:T(8,128)(2,1)}, bf16[256,1024]{1,0:T(8,128)(2,1)}, f32[256,1024]{1,0:T(8,128)S(1)}, f32[256,1024]{1,0:T(8,128)S(1)}) custom-call(s32[1,256]{1,0:T(1,128)S(1)} %get-tuple-element.106.ids_ref, bf16[256,128]{1,0:T(8,128)(2,1)S(1)} %get-tuple-element.107.first_ref, bf16[256,128]{1,0:T(8,128)(2,1)S(1)} %get-tuple-element.108.last_ref, ...), custom_call_target="tpu_custom_call" | custom-call | flops 872415232 | bytes 7222272 | tf_op jit(solution)/shard_map/cond/branch_1_fun/pallas_call | solution.py:251
  42.9 1.3 %branch_1_fun.9 = (bf16[256,1024]{1,0:T(8,128)(2,1)}, bf16[256,1024]{1,0:T(8,128)(2,1)}) custom-call(bf16[256,128]{1,0:T(8,128)(2,1)S(1)} %get-tuple-element.108.last_ref, bf16[256,1024]{1,0:T(8,128)(2,1)S(1)} %get-tuple-element.110.k_ref, bf16[256,1024]{1,0:T(8,128)(2,1)S(1)} %copy-done.7, f32[256,1024]{1,0:T(8,128)S(1)} %get-tuple-element.123.gk_in, ...), custom_call_target="tpu_custom_call" | custom-call | flops 134217728 | bytes 4521984 | tf_op jit(solution)/shard_map/cond/branch_1_fun/pallas_call | solution.py:251
  (11 shorter events, 0.0 us)
Async XLA Ops:
  0.6 0.7 %copy-start.19 = (s32[8]{0:T(128)S(1)}, s32[8]{0:T(128)}, u32[]{:S(2)}) copy-start(s32[8]{0:T(128)} %start_hbm.1) | copy-start | bytes 100
  0.6 0.7 %copy-start.16 = (s32[256]{0:T(256)S(1)}, s32[256]{0:T(256)}, u32[]{:S(2)}) copy-start(s32[256]{0:T(256)} %param.16) | copy-start | bytes 3076
  1.3 3.1 %copy-start.2 = (bf16[256,1024]{1,0:T(8,128)(2,1)S(1)}, bf16[256,1024]{1,0:T(8,128)(2,1)}, u32[]{:S(2)}) copy-start(bf16[256,1024]{1,0:T(8,128)(2,1)} %param.11) | copy-start | bytes 1572868
  1.3 3.1 %copy-start.4 = (bf16[256,1024]{1,0:T(8,128)(2,1)S(1)}, bf16[256,1024]{1,0:T(8,128)(2,1)}, u32[]{:S(2)}) copy-start(bf16[256,1024]{1,0:T(8,128)(2,1)} %k_hbm.1) | copy-start | bytes 1572868
  4.4 0.7 %copy-start.14 = (f32[1024]{0:T(1024)S(1)}, f32[1024]{0:T(1024)}, u32[]{:S(2)}) copy-start(f32[1024]{0:T(1024)} %param.15) | copy-start | bytes 12292
  5.1 10.5 %collective-permute-start.5 = (bf16[8,128,128]{2,1,0:T(8,128)(2,1)S(1)}, bf16[8,128,128]{2,1,0:T(8,128)(2,1)S(1)}, u32[]{:S(2)}, u32[]{:S(2)}) collective-permute-start(bf16[8,128,128]{2,1,0:T(8,128)(2,1)S(1)} %get-tuple-element.112), channel_id=1, source_target_pairs={{0,8},{4,12},{8,16},{12,20},{16,24},{20,28},{1,9},{5,13},{9,17},{1... | collective-permute-start | bytes 786440 | tf_op jit(solution)/shard_map/cond/branch_1_fun/ppermute | solution.py:283
  10.0 8.7 %collective-permute-start.6 = (bf16[8,128,128]{2,1,0:T(8,128)(2,1)S(1)}, bf16[8,128,128]{2,1,0:T(8,128)(2,1)S(1)}, u32[]{:S(2)}, u32[]{:S(2)}) collective-permute-start(bf16[8,128,128]{2,1,0:T(8,128)(2,1)S(1)} %get-tuple-element.115), channel_id=1, source_target_pairs={{0,4},{4,8},{8,12},{12,16},{16,20},{20,24},{24,28},{1,5},{5,9},{9,... | collective-permute-start | bytes 786440 | tf_op jit(solution)/shard_map/cond/branch_1_fun/ppermute | solution.py:283
  15.5 3.2 %copy-start.11 = (bf16[256,1024]{1,0:T(8,128)(2,1)S(1)}, bf16[256,1024]{1,0:T(8,128)(2,1)}, u32[]{:S(2)}) copy-start(bf16[256,1024]{1,0:T(8,128)(2,1)} %get-tuple-element.113.g_ref) | copy-start | bytes 1572868 | tf_op jit(solution)/shard_map/cond
  19.2 1.9 %collective-permute-start.7 = (f32[2,256]{1,0:T(2,128)S(1)}, f32[2,256]{1,0:T(2,128)S(1)}, u32[]{:S(2)}, u32[]{:S(2)}) collective-permute-start(f32[2,256]{1,0:T(2,128)S(1)} %get-tuple-element.118.refs_0_), channel_id=1, source_target_pairs={{0,1},{1,0},{2,3},{3,2},{4,5},{5,4},{6,7},{7,6},{8,9},{9,8},{10,11... | collective-permute-start | bytes 6152 | tf_op jit(solution)/shard_map/cond/branch_1_fun/ppermute | solution.py:274
  19.3 3.7 %collective-permute-start.8 = (f32[2,256]{1,0:T(2,128)S(1)}, f32[2,256]{1,0:T(2,128)S(1)}, u32[]{:S(2)}, u32[]{:S(2)}) collective-permute-start(f32[2,256]{1,0:T(2,128)S(1)} %get-tuple-element.118.refs_0_), channel_id=1, source_target_pairs={{0,2},{1,3},{2,0},{3,1},{4,6},{5,7},{6,4},{7,5},{8,10},{9,11},{10,... | collective-permute-start | bytes 6152 | tf_op jit(solution)/shard_map/cond/branch_1_fun/ppermute | solution.py:274
  20.9 3.0 %collective-permute-start.9 = (f32[2,256]{1,0:T(2,128)S(1)}, f32[2,256]{1,0:T(2,128)S(1)}, u32[]{:S(2)}, u32[]{:S(2)}) collective-permute-start(f32[2,256]{1,0:T(2,128)S(1)} %get-tuple-element.118.refs_0_), channel_id=1, source_target_pairs={{0,3},{1,2},{2,1},{3,0},{4,7},{5,6},{6,5},{7,4},{8,11},{9,10},{10,... | collective-permute-start | bytes 6152 | tf_op jit(solution)/shard_map/cond/branch_1_fun/ppermute | solution.py:274
  23.9 15.5 %copy-start.7 = (bf16[256,1024]{1,0:T(8,128)(2,1)S(1)}, bf16[256,1024]{1,0:T(8,128)(2,1)}, u32[]{:S(2)}) copy-start(bf16[256,1024]{1,0:T(8,128)(2,1)} %get-tuple-element.111.v_ref) | copy-start | bytes 1572868 | tf_op jit(solution)/shard_map/cond
  24.5 14.9 %collective-permute-start.10 = (bf16[8,128,128]{2,1,0:T(8,128)(2,1)S(1)}, bf16[8,128,128]{2,1,0:T(8,128)(2,1)S(1)}, u32[]{:S(2)}, u32[]{:S(2)}) collective-permute-start(bf16[8,128,128]{2,1,0:T(8,128)(2,1)S(1)} %get-tuple-element.120), channel_id=1, source_target_pairs={{8,0},{12,4},{16,8},{20,12},{24,16},{28,20},{9,1},{13,5},{17,9},{2... | collective-permute-start | bytes 786440 | tf_op jit(solution)/shard_map/cond/branch_1_fun/ppermute | solution.py:283
  25.8 17.1 %collective-permute-start.11 = (bf16[8,128,128]{2,1,0:T(8,128)(2,1)S(1)}, bf16[8,128,128]{2,1,0:T(8,128)(2,1)S(1)}, u32[]{:S(2)}, u32[]{:S(2)}) collective-permute-start(bf16[8,128,128]{2,1,0:T(8,128)(2,1)S(1)} %get-tuple-element.125), channel_id=1, source_target_pairs={{4,0},{8,4},{12,8},{16,12},{20,16},{24,20},{28,24},{5,1},{9,5},{13... | collective-permute-start | bytes 786440 | tf_op jit(solution)/shard_map/cond/branch_1_fun/ppermute | solution.py:283

commit v3 on v2

--- a/solution.py
+++ b/solution.py
@@ -49,34 +49,21 @@
 
 
 def tail_kernel(
-    start_hbm, ids_hbm, k_hbm, v_hbm,
-    tail_ref, tail2_ref, first_ref, last_ref, needs_ref, plan_ref,
-    start_ref, ids_ref, k_ref, v_ref, sems,
+    start_hbm, ids_hbm, k_hbm, v_hbm, gain_hbm,
+    tail_ref, tail2_ref, first_ref, last_ref, needs_ref, ids_ref, gain_ref, k_ref, v_ref, plan_ref,
+    start_ref, sems,
 ):
-    chunks = k_ref.shape[0]
-    cols = k_ref.shape[2]
-    small = [
-        pltpu.make_async_copy(ids_hbm, ids_ref, sems.at[2 * chunks]),
-        pltpu.make_async_copy(start_hbm, start_ref, sems.at[2 * chunks + 1]),
-    ]
-    large = []
-    for i in range(chunks):
-        at = pl.ds(i * cols, cols)
-        large.append((
-            pltpu.make_async_copy(k_hbm.at[:, at], k_ref.at[i], sems.at[2 * i]),
-            pltpu.make_async_copy(v_hbm.at[:, at], v_ref.at[i], sems.at[2 * i + 1]),
-        ))
-    for copy in small:
+    pairs = (start_hbm, start_ref), (ids_hbm, ids_ref), (k_hbm, k_ref), (v_hbm, v_ref), (gain_hbm, gain_ref)
+    copies = [pltpu.make_async_copy(*pair, sems.at[i]) for i, pair in enumerate(pairs)]
+    for copy in copies:
         copy.start()
-    for pair in large:
-        for copy in pair:
-            copy.start()
-    for copy in small:
+    for copy in copies[:2]:
         copy.wait()
     me, top = lax.axis_index("seq"), start_ref.shape[0] - 1
     blocks, pairs = jnp.int32(0), jnp.int32(0)
     for c in range(top + 1):
         begin = start_ref[c]
+        plan_ref[1 + c] = begin
         blocks = jnp.maximum(blocks, c - begin)
         pairs = jnp.maximum(pairs, c // 2 - (begin >> 1))
     plan_ref[0] = jnp.where(blocks <= 2, jnp.maximum(blocks - 1, 0), jnp.where(pairs <= 1, PAIRS, ANY))
@@ -90,30 +77,29 @@
     last = (col == row[:, -1:]).astype(f32)
     last_ref[...] = wide(last)
     last = wide(last * jnp.where(need, 1.0, 0.0))
-    for i, pair in enumerate(large):
-        for copy in pair:
-            copy.wait()
-        for j in range(cols // HD):
-            state = dot(k_ref[i, :, head_cols(j)] * last, v_ref[i, :, head_cols(j)], 0, 0)
-            h = i * (cols // HD) + j
-            tail_ref[h] = state.astype(bf16)
-            tail2_ref[h] = jnp.where(need2, state, 0.0).astype(bf16)
-
-
-def local_kernel(ids_ref, first_ref, q_ref, k_ref, v_ref, *refs):
-    far_refs, att_ref = refs[:-1], refs[-1]
+    for copy in copies[2:]:
+        copy.wait()
+    for h in range(tail_ref.shape[0]):
+        state = dot(k_ref[:, head_cols(h)] * last, v_ref[:, head_cols(h)], 0, 0)
+        tail_ref[h] = state.astype(bf16)
+        tail2_ref[h] = jnp.where(need2, state, 0.0).astype(bf16)
+
+
+def local_kernel(q_hbm, g_hbm, ids_ref, k_ref, v_ref, att_ref, q_ref, g_ref, sems):
+    copies = [pltpu.make_async_copy(*pair, sems.at[i]) for i, pair in enumerate(((q_hbm, q_ref), (g_hbm, g_ref)))]
+    for copy in copies:
+        copy.start()
     row, col = ids_of(ids_ref)
     n = row.shape[1]
     t = lax.broadcasted_iota(jnp.int32, (n, n), 0)
     u = lax.broadcasted_iota(jnp.int32, (n, n), 1)
     same = (u <= t) & (col == row)
+    for copy in copies:
+        copy.wait()
     for h in range(q_ref.shape[1] // HD):
         c = head_cols(h)
         w = jnp.where(same, dot(q_ref[:, c], k_ref[:, c], 1, 1), 0.0).astype(bf16)
-        att = dot(w, v_ref[:, c], 1, 0)
-        for far_ref in far_refs:
-            att = att + dot(q_ref[:, c] * first_ref[...], far_ref[h], 1, 0)
-        att_ref[:, c] = att
+        att_ref[:, c] = dot(w, v_ref[:, c], 1, 0)
 
 
 def joined(plan, way, refs, h):
@@ -189,9 +175,8 @@
             ref[h] = jnp.where(need, state, 0.0).astype(bf16)
 
 
-def back_kernel(plan, n_sums, n_far, ids_ref, first_ref, last_ref, att_ref, q_ref, k_ref, v_ref, grad_ref, gain_ref, *refs):
-    sum_refs, refs, (normed_ref, gq_ref, gk_ref, gv_ref) = refs[:n_sums], refs[n_sums:-4], refs[-4:]
-    far_refs, state_refs = refs[:n_far], refs[n_far:]
+def back_kernel(plan, n_sums, ids_ref, first_ref, att_ref, q_ref, k_ref, v_ref, grad_ref, gain_ref, *refs):
+    sum_refs, state_refs, (normed_ref, gq_ref, gk_ref, gv_ref) = refs[:n_sums], refs[n_sums:-4], refs[-4:]
     inverse = column(scales(sum_refs)[0])
     row, col = ids_of(ids_ref)
     first = first_ref[...]
@@ -207,14 +192,17 @@
         gs = jnp.where(same, dot(grad, v, 1, 1), 0.0).astype(bf16)
         gq_ref[:, c] = (dot(gs, k, 1, 0) + dot(grad * first, joined(plan, 1, state_refs, h), 1, 1)).astype(bf16)
         gs_t = jnp.where(same_t, dot(v, grad, 1, 1), 0.0).astype(bf16)
-        gk = dot(gs_t, q, 1, 0)
+        gk_ref[:, c] = dot(gs_t, q, 1, 0)
         w_t = jnp.where(same_t, dot(k, q, 1, 1), 0.0).astype(bf16)
-        gv = dot(w_t, grad, 1, 0)
-        for far_ref in far_refs:
-            gk = gk + dot(v * last_ref[...], far_ref[h], 1, 1)
-            gv = gv + dot(k * last_ref[...], far_ref[h], 1, 0)
-        gk_ref[:, c] = gk
-        gv_ref[:, c] = gv
+        gv_ref[:, c] = dot(w_t, grad, 1, 0)
+
+
+def add_kernel(last_ref, k_ref, v_ref, state_ref, gk_in, gv_in, gk_ref, gv_ref):
+    last = last_ref[...]
+    for h in range(k_ref.shape[1] // HD):
+        c = head_cols(h)
+        gk_ref[:, c] = gk_in[:, c] + dot(v_ref[:, c] * last, state_ref[h], 1, 1)
+        gv_ref[:, c] = gv_in[:, c] + dot(k_ref[:, c] * last, state_ref[h], 1, 0)
 
 
 def last_kernel(plan, last_ref, k_ref, v_ref, gk_in, gv_in, *refs):
@@ -242,6 +230,10 @@
     return jax.ShapeDtypeStruct(a.shape, a.dtype)
 
 
+def in_hbm(a):
+    return pltpu.with_memory_space_constraint(a, pltpu.HBM)
+
+
 def call(kernel, outs, flops, *args, in_space=None, out_space=None, scratch=()):
     moved = sum(a.size * a.dtype.itemsize for a in (*args, *outs))
 
@@ -251,7 +243,7 @@
     return pl.pallas_call(
         kernel,
         out_shape=outs,
-        in_specs=[spec(a, in_space) for a in args],
+        in_specs=[spec(a, space) for a, space in zip(args, in_space or [None] * len(args))],
         out_specs=tuple(spec(a, out_space) for a in outs),
         scratch_shapes=scratch,
         cost_estimate=pl.CostEstimate(flops=flops, bytes_accessed=moved, transcendentals=0),
@@ -300,7 +292,7 @@
     return [spread(state, reach if way == 1 else reach.T, groups)]
 
 
-def layer(plan, tail, tail2, first, last, needs, query_in, key_in, value_in, out_grad, gain, ids, start_group):
+def layer(plan, tail, tail2, first, last, needs, ids, gain, key_in, value_in, plan_and_start, query_in, out_grad):
     n, cols = query_in.shape
     heads = cols // HD
     tokens = shape_of(query_in)
@@ -308,14 +300,21 @@
     square = 2 * heads * n * n * HD
     narrow = 2 * heads * n * HD * HD
 
+    start_group = plan_and_start[1:]
     earlier = exchange(plan, 1, [tail, tail2] if plan == TWO else [tail], start_group)
-    near, far = (earlier[:1], earlier[1:]) if plan == TWO else (earlier, [])
-    (att_local,) = call(local_kernel, (tokens32,), 2 * square, ids, first, query_in, key_in, value_in, *far)
+    att_local, query_in, out_grad = call(
+        local_kernel,
+        (tokens32, tokens, tokens),
+        2 * square,
+        in_hbm(query_in), in_hbm(out_grad), ids, key_in, value_in,
+        in_space=[pltpu.HBM] * 2 + [pltpu.VMEM] * 3,
+        scratch=[pltpu.SemaphoreType.DMA((2,))],
+    )
     att, sums = call(
         functools.partial(attend_kernel, plan),
         (tokens32, jax.ShapeDtypeStruct((2, n), f32)),
         narrow,
-        first, att_local, query_in, out_grad, gain, *near,
+        first, att_local, query_in, out_grad, gain, *earlier,
     )
     sums = over_head(sums)
     n_heads = 2 if plan == TWO else 1
@@ -326,20 +325,23 @@
         needs, first, att, query_in, out_grad, gain, *sums,
     )
     later = exchange(plan, -1, head_states, start_group)
-    near, far = (later[:1], later[1:]) if plan == TWO else (later, [])
     normed, grad_query, gk, gv = call(
-        functools.partial(back_kernel, plan, len(sums), len(far)),
+        functools.partial(back_kernel, plan, len(sums)),
         (tokens, tokens, tokens32, tokens32),
         6 * square + narrow,
-        ids, first, last, att, query_in, key_in, value_in, grad, gain, *sums, *far, *earlier,
+        ids, first, att, query_in, key_in, value_in, grad, gain, *sums, *earlier,
     )
     chunks = 4 if heads % 4 == 0 else 1
     part = pltpu.VMEM((chunks, n, cols // chunks), bf16)
+    if plan == TWO:
+        near, far = later
+        gk, gv = call(add_kernel, (tokens32, tokens32), 2 * narrow, last, key_in, value_in, far, gk, gv)
+        later = [near]
     grad_key, grad_value = call(
         functools.partial(last_kernel, plan),
         (tokens, tokens),
         2 * narrow,
-        last, key_in, value_in, gk, gv, *near,
+        last, key_in, value_in, gk, gv, *later,
         out_space=pltpu.HBM,
         scratch=[part, part, pltpu.SemaphoreType.DMA((2 * chunks,))],
     )
@@ -352,29 +354,23 @@
     ids, gain = doc_ids.reshape(1, n), norm_gain.reshape(1, cols)
     state = jax.ShapeDtypeStruct((heads, HD, HD), bf16)
     mask = jax.ShapeDtypeStruct((n, HD), bf16)
-    chunks = 4 if heads % 4 == 0 else 1
-    part = pltpu.VMEM((chunks, n, cols // chunks), bf16)
     *held, plan = call(
         tail_kernel,
         (
             state, state, mask, mask,
-            jax.ShapeDtypeStruct((2, HD), f32), jax.ShapeDtypeStruct((1,), jnp.int32),
+            jax.ShapeDtypeStruct((2, HD), f32), shape_of(ids), shape_of(gain), shape_of(key_in), shape_of(value_in),
+            jax.ShapeDtypeStruct((1 + start_group.shape[0],), jnp.int32),
         ),
         2 * heads * n * HD * HD,
-        start_group, ids, key_in, value_in,
-        in_space=pltpu.HBM,
-        scratch=[
-            pltpu.SMEM(start_group.shape, jnp.int32),
-            pltpu.VMEM((1, n), jnp.int32),
-            part, part,
-            pltpu.SemaphoreType.DMA((2 * chunks + 2,)),
-        ],
+        *map(in_hbm, (start_group, ids, key_in, value_in, gain)),
+        in_space=[pltpu.HBM] * 5,
+        scratch=[pltpu.SMEM(start_group.shape, jnp.int32), pltpu.SemaphoreType.DMA((5,))],
     )
     plans = (ONE, TWO, PAIRS if start_group.shape[0] % 4 == 0 else ANY, ANY)
     return lax.switch(
         plan[0],
         [functools.partial(layer, way) for way in plans],
-        *held, query_in, key_in, value_in, out_grad, gain, ids, start_group,
+        *held, plan, query_in, out_grad,
     )
 
 

time: 45.1 us -> 31.6 us (0.70)
  waiting for transfers between devices: 18 us -> 11.8 us
  starting transfers between devices: 12.9 us -> 8.1 us
  local copies, waits for them, and re-layouts: 1.36 us -> 0 us
  between operations: 1.51 us -> 0.86 us
    ppermute x4 -> x2, waiting for transfers between devices: 15.3 us -> 10 us  [exchange(): lax.ppermute(state, 'seq', [(i, i + way * k) for i in range(groups) if 0...]
    ppermute x4 -> x2, starting transfers between devices: 11 us -> 6.18 us  [exchange(): lax.ppermute(state, 'seq', [(i, i + way * k) for i in range(groups) if 0...]
    unnamed x10 -> x0, local copies, waits for them, and re-layouts: 1.35 us -> none
    ppermute x3, waiting for transfers between devices: 2.7 us -> 1.8 us  [over_head(): lax.ppermute(sums, 'head', [(i, i ^ k if power else (i + k) % size) for i...]
  transfers between devices with their start and end apart: 7 -> 5, of which waited for: 5 -> 4; matrix products, arithmetic and copies ran while one was open for 0% -> 0% of each run, Pallas kernels for 13% -> 18%
where the time goes in v3:
time: 31.6 us; the launch traced here: 31.4 us
  waiting for transfers between devices  11.8 us (37%)
  Pallas kernels  10.3 us (33%)
  starting transfers between devices  8.1 us (26%)
  between operations  0.86 us (3%)
    pallas_call x6, Pallas kernels, call(): pl.pallas_call(kernel, out_shape=outs, in_specs=[spec(a, space) for a, sp...  10.3 us
    ppermute x2, waiting for transfers between devices, exchange(): lax.ppermute(state, 'seq', [(i, i + way * k) for i in range(groups) if 0...  10 us
    ppermute x2, starting transfers between devices, exchange(): lax.ppermute(state, 'seq', [(i, i + way * k) for i in range(groups) if 0...  6.18 us
    ppermute x3, starting transfers between devices, over_head(): lax.ppermute(sums, 'head', [(i, i ^ k if power else (i + k) % size) for i...  1.93 us
    ppermute x3, waiting for transfers between devices, over_head(): lax.ppermute(sums, 'head', [(i, i ^ k if power else (i + k) % size) for i...  1.8 us
  transfers between devices with their start and end apart: 5, of which 4 were waited for; matrix products, arithmetic and copies ran while one was open for 0% of the time, Pallas kernels for 18%

profile of v3, /device:TPU:0, one launch (start us, length us, event | category | flops | bytes accessed | tf_op | source)
XLA Modules:
  0.0 31.4 jit_solution(2742414961540575377)
XLA Ops:
  0.6 2.3 %shard_map.102 = (bf16[8,128,128]{2,1,0:T(8,128)(2,1)}, bf16[8,128,128]{2,1,0:T(8,128)(2,1)S(1)}, bf16[256,128]{1,0:T(8,128)(2,1)S(1)}, bf16[256,128]{1,0:T(8,12...) custom-call(s32[8]{0:T(128)} %start_hbm.1, ...), custom_call_target="tpu_custom_call" | custom-call | flops 67108864 | bytes 2763844 | tf_op jit(solution)/shard_map/pallas_call | solution.py:243
  3.0 28.2 %conditional.1 = (bf16[256,1024]{1,0:T(8,128)(2,1)}, bf16[256,1024]{1,0:T(8,128)(2,1)}, bf16[256,1024]{1,0:T(8,128)(2,1)}, bf16[256,1024]{1,0:T(8,128)(2,1)}) conditional(s32[]{:T(128)} %bitcast.4, (bf16[256,1024]{1,0:T(8,128)(2,1)}, bf16[256,1024]{1,0:T(8,128)(2,1)}, s32[1,256]{1,0:T(1,128)S(1)}, ...), branch_computations={%region_0.0_spmd, %region_1.0_spmd, %region_2.0_spmd, %region_3.0_... | conditional | flops 1543503872 | bytes 43615888 | solution.py:370
  3.0 4.9 %collective-permute-start = (bf16[8,128,128]{2,1,0:T(8,128)(2,1)}, bf16[8,128,128]{2,1,0:T(8,128)(2,1)S(1)}, u32[]{:S(2)}, u32[]{:S(2)}) collective-permute-start(bf16[8,128,128]{2,1,0:T(8,128)(2,1)} %get-tuple-element.96), channel_id=1, source_target_pairs={{0,4},{4,8},{8,12},{12,16},{16,20},{20,24},{24,28},{1,5},{5,9},{9,... | collective-permute-start | bytes 786440 | tf_op jit(solution)/shard_map/cond/branch_0_fun/ppermute | solution.py:275
  7.9 2.2 %branch_0_fun.5 = (f32[256,1024]{1,0:T(8,128)S(1)}, bf16[256,1024]{1,0:T(8,128)(2,1)S(1)}, bf16[256,1024]{1,0:T(8,128)(2,1)S(1)}) custom-call(bf16[256,1024]{1,0:T(8,128)(2,1)} %get-tuple-element.88.q_hbm, bf16[256,1024]{1,0:T(8,128)(2,1)} %get-tuple-element.89.g_hbm, s32[1,256]{1,0:T(1,128)S(1)} %get-tuple-element.86.ids_ref, ...), custom_call_target="tpu_custom_call" | custom-call | flops 268435456 | bytes 4195328 | tf_op jit(solution)/shard_map/cond/branch_0_fun/pallas_call | solution.py:243
  10.1 3.7 %collective-permute-done.refs_0_.refs_4_ = bf16[8,128,128]{2,1,0:T(8,128)(2,1)S(1)} collective-permute-done((bf16[8,128,128]{2,1,0:T(8,128)(2,1)}, bf16[8,128,128]{2,1,0:T(8,128)(2,1)S(1)}, u32[]{:S(2)}, u32[]{:S(2)}) %collective-permute-start) | collective-permute-done | bytes 262176 | tf_op jit(solution)/shard_map/cond/branch_0_fun/ppermute | solution.py:275
  13.8 0.5 %branch_0_fun.6 = (f32[256,1024]{1,0:T(8,128)S(1)}, f32[2,256]{1,0:T(2,128)S(1)}) custom-call(bf16[256,128]{1,0:T(8,128)(2,1)S(1)} %get-tuple-element.87.first_ref, f32[256,1024]{1,0:T(8,128)S(1)} %get-tuple-element.92.att_ref, bf16[256,1024]{1,0:T(8,128)(2,1)S(1)} %get-tuple-element.93.q_ref, bf16[256,1024]{1,0:T(8,128)(2,1)S(1)} %get-tuple-element.94.g_ref, ...), custom_call_target="tpu_custom_call" | custom-call | flops 67108864 | bytes 3479552 | tf_op jit(solution)/shard_map/cond/branch_0_fun/pallas_call | solution.py:243
  14.3 0.1 collective-permute-start.3
  14.4 1.5 %collective-permute-start.2 = (f32[2,256]{1,0:T(2,128)S(1)}, f32[2,256]{1,0:T(2,128)S(1)}, u32[]{:S(2)}, u32[]{:S(2)}) collective-permute-start(f32[2,256]{1,0:T(2,128)S(1)} %get-tuple-element.99.refs_0_), channel_id=1, source_target_pairs={{0,2},{1,3},{2,0},{3,1},{4,6},{5,7},{6,4},{7,5},{8,10},{9,11},{10,... | collective-permute-start | bytes 6152 | tf_op jit(solution)/shard_map/cond/branch_0_fun/ppermute | solution.py:266
  15.9 0.3 collective-permute-start.1
  16.2 1.1 %collective-permute-done.3.refs_3_ = f32[2,256]{1,0:T(2,128)S(1)} collective-permute-done((f32[2,256]{1,0:T(2,128)S(1)}, f32[2,256]{1,0:T(2,128)S(1)}, u32[]{:S(2)}, u32[]{:S(2)}) %collective-permute-start.3) | collective-permute-done | bytes 2080 | tf_op jit(solution)/shard_map/cond/branch_0_fun/ppermute | solution.py:266
  17.4 0.7 %collective-permute-done.2.refs_2_ = f32[2,256]{1,0:T(2,128)S(1)} collective-permute-done((f32[2,256]{1,0:T(2,128)S(1)}, f32[2,256]{1,0:T(2,128)S(1)}, u32[]{:S(2)}, u32[]{:S(2)}) %collective-permute-start.2) | collective-permute-done | bytes 2080 | tf_op jit(solution)/shard_map/cond/branch_0_fun/ppermute | solution.py:266
  18.0 0.0 collective-permute-done.1.refs_1_
  18.0 0.6 %branch_0_fun.7 = (bf16[256,1024]{1,0:T(8,128)(2,1)S(1)}, bf16[8,128,128]{2,1,0:T(8,128)(2,1)S(1)}) custom-call(f32[2,128]{1,0:T(2,128)S(1)} %get-tuple-element.98.needs_ref, bf16[256,128]{1,0:T(8,128)(2,1)S(1)} %get-tuple-element.87.first_ref, f32[256,1024]{1,0:T(8,128)S(1)} %get-tuple-element.97.att_ref, bf16[256,1024]{1,0:T(8,128)(2,1)S(1)} %get-tuple-element.93.q_ref, ...), custom_call_target="tpu_custom_call" | custom-call | flops 67108864 | bytes 2962432 | tf_op jit(solution)/shard_map/cond/branch_0_fun/pallas_call | solution.py:243
  18.6 1.3 %collective-permute-start.4 = (bf16[8,128,128]{2,1,0:T(8,128)(2,1)S(1)}, bf16[8,128,128]{2,1,0:T(8,128)(2,1)S(1)}, u32[]{:S(2)}, u32[]{:S(2)}) collective-permute-start(bf16[8,128,128]{2,1,0:T(8,128)(2,1)S(1)} %get-tuple-element.106), channel_id=1, source_target_pairs={{4,0},{8,4},{12,8},{16,12},{20,16},{24,20},{28,24},{5,1},{9,5},{13... | collective-permute-start | bytes 786440 | tf_op jit(solution)/shard_map/cond/branch_0_fun/ppermute | solution.py:275
  19.9 3.5 %branch_0_fun.8 = (bf16[256,1024]{1,0:T(8,128)(2,1)}, bf16[256,1024]{1,0:T(8,128)(2,1)}, f32[256,1024]{1,0:T(8,128)S(1)}, f32[256,1024]{1,0:T(8,128)S(1)}) custom-call(s32[1,256]{1,0:T(1,128)S(1)} %get-tuple-element.86.ids_ref, bf16[256,128]{1,0:T(8,128)(2,1)S(1)} %get-tuple-element.87.first_ref, f32[256,1024]{1,0:T(8,128)S(1)} %get-tuple-element.97.att_ref, ...), custom_call_target="tpu_custom_call" | custom-call | flops 872415232 | bytes 6632448 | tf_op jit(solution)/shard_map/cond/branch_0_fun/pallas_call | solution.py:243
  23.4 6.4 %collective-permute-done.4.refs_0_ = bf16[8,128,128]{2,1,0:T(8,128)(2,1)S(1)} collective-permute-done((bf16[8,128,128]{2,1,0:T(8,128)(2,1)S(1)}, bf16[8,128,128]{2,1,0:T(8,128)(2,1)S(1)}, u32[]{:S(2)}, u32[]{:S(2)}) %collective-permute-start.4) | collective-permute-done | bytes 262176 | tf_op jit(solution)/shard_map/cond/branch_0_fun/ppermute | solution.py:275
  29.7 1.3 %branch_0_fun.9 = (bf16[256,1024]{1,0:T(8,128)(2,1)}, bf16[256,1024]{1,0:T(8,128)(2,1)}) custom-call(bf16[256,128]{1,0:T(8,128)(2,1)S(1)} %get-tuple-element.103.last_ref, bf16[256,1024]{1,0:T(8,128)(2,1)S(1)} %get-tuple-element.90.k_ref, bf16[256,1024]{1,0:T(8,128)(2,1)S(1)} %get-tuple-element.91.v_ref, f32[256,1024]{1,0:T(8,128)S(1)} %get-tuple-element.104.gk_in, ...), custom_call_target="tpu_custom_call" | custom-call | flops 134217728 | bytes 4521984 | tf_op jit(solution)/shard_map/cond/branch_0_fun/pallas_call | solution.py:243
Async XLA Ops:
  3.0 10.7 %collective-permute-start = (bf16[8,128,128]{2,1,0:T(8,128)(2,1)}, bf16[8,128,128]{2,1,0:T(8,128)(2,1)S(1)}, u32[]{:S(2)}, u32[]{:S(2)}) collective-permute-start(bf16[8,128,128]{2,1,0:T(8,128)(2,1)} %get-tuple-element.96), channel_id=1, source_target_pairs={{0,4},{4,8},{8,12},{12,16},{16,20},{20,24},{24,28},{1,5},{5,9},{9,... | collective-permute-start | bytes 786440 | tf_op jit(solution)/shard_map/cond/branch_0_fun/ppermute | solution.py:275
  14.3 3.1 %collective-permute-start.3 = (f32[2,256]{1,0:T(2,128)S(1)}, f32[2,256]{1,0:T(2,128)S(1)}, u32[]{:S(2)}, u32[]{:S(2)}) collective-permute-start(f32[2,256]{1,0:T(2,128)S(1)} %get-tuple-element.99.refs_0_), channel_id=1, source_target_pairs={{0,3},{1,2},{2,1},{3,0},{4,7},{5,6},{6,5},{7,4},{8,11},{9,10},{10,... | collective-permute-start | bytes 6152 | tf_op jit(solution)/shard_map/cond/branch_0_fun/ppermute | solution.py:266
  14.4 3.6 %collective-permute-start.2 = (f32[2,256]{1,0:T(2,128)S(1)}, f32[2,256]{1,0:T(2,128)S(1)}, u32[]{:S(2)}, u32[]{:S(2)}) collective-permute-start(f32[2,256]{1,0:T(2,128)S(1)} %get-tuple-element.99.refs_0_), channel_id=1, source_target_pairs={{0,2},{1,3},{2,0},{3,1},{4,6},{5,7},{6,4},{7,5},{8,10},{9,11},{10,... | collective-permute-start | bytes 6152 | tf_op jit(solution)/shard_map/cond/branch_0_fun/ppermute | solution.py:266
  15.9 2.1 %collective-permute-start.1 = (f32[2,256]{1,0:T(2,128)S(1)}, f32[2,256]{1,0:T(2,128)S(1)}, u32[]{:S(2)}, u32[]{:S(2)}) collective-permute-start(f32[2,256]{1,0:T(2,128)S(1)} %get-tuple-element.99.refs_0_), channel_id=1, source_target_pairs={{0,1},{1,0},{2,3},{3,2},{4,5},{5,4},{6,7},{7,6},{8,9},{9,8},{10,11... | collective-permute-start | bytes 6152 | tf_op jit(solution)/shard_map/cond/branch_0_fun/ppermute | solution.py:266
  18.6 11.1 %collective-permute-start.4 = (bf16[8,128,128]{2,1,0:T(8,128)(2,1)S(1)}, bf16[8,128,128]{2,1,0:T(8,128)(2,1)S(1)}, u32[]{:S(2)}, u32[]{:S(2)}) collective-permute-start(bf16[8,128,128]{2,1,0:T(8,128)(2,1)S(1)} %get-tuple-element.106), channel_id=1, source_target_pairs={{4,0},{8,4},{12,8},{16,12},{20,16},{24,20},{28,24},{5,1},{9,5},{13... | collective-permute-start | bytes 786440 | tf_op jit(solution)/shard_map/cond/branch_0_fun/ppermute | solution.py:275
